TPU v7x, 768 devices: a whole 4x8x12 slice. The times are simulated.
768 devices in a mesh: rows: 96 (over z, x, core), rep: 8 (over y).
Axes of the slice: x: 4, y: 8, z: 12, core: 2. Of those that a mesh axis runs over, the one named last changes fastest.
Arguments:
- block_values: bfloat16 [1536, 8, 64, 64], P('rows'), may hold values from -0.8984375 to 0.8984375
- pattern_cols: int32 [1536, 8], replicated, may hold values from 0 to 1535, as said below
- pattern_counts: int32 [1536], replicated, may hold values from 4 to 8, as said below
Outputs:
- purified: bfloat16 [1536, 8, 64, 64], P('rows', 'rep')
Inputs may be any that keep to these rules, and one draw needn't show every extreme that they name: `pattern_cols`: slot 0 of block row i holds i, slot 1 holds i + 8 or i - 8 modulo 1536, every column of row i lies within 8 of i modulo 1536, and the columns of a row are distinct. Only slots below pattern_counts[i] hold blocks of the matrix; some block row uses all 8 slots.
All inputs are finite; a program needn't handle non-finite values.
Results may differ from a plain program's by a relative error of at most 0.0049.
Values may be sent and summed in bfloat16 or wider, within the bound.
No kernel may reach another device: no remote copies, remote signals or barrier semaphores. Data moves between devices by JAX's collectives and lax.ppermute only.
A program may use at most 32 MiB of HBM per device.

v0:
```python
import jax
import jax.numpy as jnp
from jax import lax
from jax.sharding import PartitionSpec as P


def with_halo(block, sides, width):
    for axis, dim in sides:
        count = lax.axis_size(axis)
        forward = [(i, i + 1) for i in range(count - 1)]
        forward.append((count - 1, 0))
        backward = [(target, source) for source, target in forward]
        low = lax.ppermute(
            lax.slice_in_dim(block, block.shape[dim] - width, None, axis=dim), axis, forward
        )
        high = lax.ppermute(lax.slice_in_dim(block, 0, width, axis=dim), axis, backward)
        block = jnp.concatenate([low, block, high], axis=dim)
    return block


def lookup(values, pattern_cols, pattern_counts, row_ids, slot_ids, anchor, halo_reach):
    total_rows = pattern_cols.shape[0]
    slot_count = pattern_cols.shape[1]
    block_side = values.shape[-1]
    own_cols = jnp.take(pattern_cols, row_ids, axis=0)
    own_count = jnp.take(pattern_counts, row_ids, axis=0)
    target = jnp.take(own_cols, slot_ids, axis=1)
    far_cols = jnp.take(pattern_cols, own_cols, axis=0)
    far_count = jnp.take(pattern_counts, own_cols, axis=0)
    position = jnp.arange(slot_count, dtype=jnp.int32)
    matched = (far_cols[:, None, :, :] == target[:, :, None, None]) & (
        position[None, None, None, :] < far_count[:, None, :, None]
    )
    located = (
        jnp.any(matched, axis=3)
        & (position[None, None, :] < own_count[:, None, None])
        & (slot_ids[None, :, None] < own_count[:, None, None])
    )
    where_at = jnp.sum(jnp.where(matched, position[None, None, None, :], 0), axis=3)
    local_row = (own_cols - anchor + halo_reach) % total_rows
    flat_index = local_row[:, None, :] * slot_count + where_at
    blocks = jnp.take(values.reshape(-1, block_side, block_side), flat_index, axis=0)
    return jnp.where(located[..., None, None], blocks, jnp.zeros((), values.dtype))


def purify(square, cube):
    return (3.0 * square.astype(jnp.float32) - 2.0 * cube).astype(jnp.bfloat16)


def local(block_values, pattern_cols, pattern_counts):
    rows_here = block_values.shape[0]
    slot_count = block_values.shape[1]
    halo_reach = rows_here // 2
    anchor = lax.axis_index("rows") * rows_here
    rep_count = lax.axis_size("rep")
    rep_index = lax.axis_index("rep")
    slot_share = slot_count // rep_count
    extended = with_halo(block_values, (("rows", 0),), halo_reach)
    row_ids = anchor + jnp.arange(rows_here, dtype=jnp.int32)
    my_slots = rep_index * slot_share + jnp.arange(slot_share, dtype=jnp.int32)
    gathered = lookup(extended, pattern_cols, pattern_counts, row_ids, my_slots, anchor, halo_reach)
    square = jnp.einsum(
        "ibxy,iabyz->iaxz", block_values, gathered, preferred_element_type=jnp.float32
    ).astype(jnp.bfloat16)
    cube = jnp.einsum(
        "ibxy,iabyz->iaxz",
        lax.all_gather(square, "rep", axis=1, tiled=True),
        gathered,
        preferred_element_type=jnp.float32,
    )
    return purify(square, cube)


def solution(mesh):
    in_specs = (P("rows", None, None, None), P(), P())
    out_specs = P("rows", "rep", None, None)
    return jax.shard_map(local, mesh=mesh, in_specs=in_specs, out_specs=out_specs, check_vma=False)
```

profile of v0, /device:TPU:2, one launch (start us, length us, event | category | flops | bytes accessed | tf_op | source)
XLA Modules:
  0.0 108.6 jit_solution(14337160600809887980)
XLA Ops:
  6.5 2.8 %fusion.43 = (bf16[8,8,64,64]{3,2,1,0:T(8,128)(2,1)}, bf16[8,8,64,64]{3,2,1,0:T(8,128)(2,1)S(1)}) fusion(bf16[16,8,64,64]{3,2,1,0:T(8,128)(2,1)} %param.3), kind=kLoop, calls=%fused_computation.65 | loop fusion | bytes 2097152 | tf_op jit(solution)/shard_map/slice | solution.py:14
  9.3 1.9 %collective-permute-start = (bf16[8,8,64,64]{3,2,1,0:T(8,128)(2,1)}, bf16[8,8,64,64]{3,2,1,0:T(8,128)(2,1)}, u32[]{:S(2)}, u32[]{:S(2)}) collective-permute-start(bf16[8,8,64,64]{3,2,1,0:T(8,128)(2,1)} %get-tuple-element.23), channel_id=1, source_target_pairs={{0,8},{8,16},{16,24},{24,32},{32,40},{40,48},{48,56},{56,64},{64,7... | collective-permute-start | bytes 1572872 | tf_op jit(solution)/shard_map/ppermute | solution.py:13
  11.2 3.6 %collective-permute-start.1 = (bf16[8,8,64,64]{3,2,1,0:T(8,128)(2,1)S(1)}, bf16[8,8,64,64]{3,2,1,0:T(8,128)(2,1)}, u32[]{:S(2)}, u32[]{:S(2)}) collective-permute-start(bf16[8,8,64,64]{3,2,1,0:T(8,128)(2,1)S(1)} %get-tuple-element.24), channel_id=1, source_target_pairs={{8,0},{16,8},{24,16},{32,24},{40,32},{48,40},{56,48},{64,56},{72,6... | collective-permute-start | bytes 1572872 | tf_op jit(solution)/shard_map/ppermute | solution.py:16
  14.9 0.3 copy.24
  15.2 0.0 copy-done
  15.2 0.7 gather_fusion.3
  15.9 0.6 gather_fusion
  16.4 0.1 copy.25
  16.5 0.1 copy.26
  16.6 0.1 reshape.361
  16.7 0.6 gather_fusion.1
  17.4 1.1 %gather_fusion.2 = s32[128]{0:T(128)S(1)} fusion(s32[1536]{0:T(1024)S(1)} %copy-done, s32[1024]{0:T(1024)S(1)} %pad_clamp_fusion.1), kind=kCustom, calls=%fused_computation.2 | custom fusion | bytes 1536 | tf_op jit(solution)/shard_map/jit(_take)/gather | solution.py:29
  18.5 0.1 reshape.368
  18.6 0.1 broadcast_select_fusion
  18.7 0.2 select_reduce_fusion.1
  18.9 0.4 fusion.41
  19.3 0.3 select_reduce_fusion
  19.7 0.1 copy.29
  19.8 0.1 copy.30
  19.8 0.1 reshape.385
  19.9 0.1 fusion.30
  20.0 5.7 %collective-permute-done = bf16[8,8,64,64]{3,2,1,0:T(8,128)(2,1)} collective-permute-done((bf16[8,8,64,64]{3,2,1,0:T(8,128)(2,1)}, bf16[8,8,64,64]{3,2,1,0:T(8,128)(2,1)}, u32[]{:S(2)}, u32[]{:S(2)}) %collective-permute-start) | collective-permute-done | bytes 524320 | tf_op jit(solution)/shard_map/ppermute | solution.py:13
  25.7 1.4 %collective-permute-done.1 = bf16[8,8,64,64]{3,2,1,0:T(8,128)(2,1)} collective-permute-done((bf16[8,8,64,64]{3,2,1,0:T(8,128)(2,1)S(1)}, bf16[8,8,64,64]{3,2,1,0:T(8,128)(2,1)}, u32[]{:S(2)}, u32[]{:S(2)}) %collective-permute-start.1) | collective-permute-done | bytes 524320 | tf_op jit(solution)/shard_map/ppermute | solution.py:16
  27.2 3.7 %pad_maximum_fusion = bf16[32,8,64,64]{3,2,1,0:T(8,128)(2,1)} fusion(bf16[8,8,64,64]{3,2,1,0:T(8,128)(2,1)} %collective-permute-done.1, bf16[16,8,64,64]{3,2,1,0:T(8,128)(2,1)S(1)} %copy-done.1, bf16[8,8,64,64]{3,2,1,0:T(8,128)(2,1)} %collective-permute-done), kind=kLoop, calls=%fused_computation.5 | loop fusion | flops 2097152 | bytes 4194304 | tf_op jit(solution)/shard_map/concatenate | solution.py:17
  30.9 3.1 %gather_fusion.4 = bf16[128,64,64]{2,1,0:T(8,128)(2,1)S(1)} fusion(bf16[256,64,64]{2,1,0:T(8,128)(2,1)} %bitcast.67, s32[1024]{0:T(1024)S(1)} %pad_clamp_fusion), kind=kCustom, calls=%fused_computation.4 | custom fusion | bytes 2097664 | tf_op jit(solution)/shard_map/jit(_take)/gather | solution.py:42
  34.0 2.8 %copy.31 = bf16[128,64,64]{1,2,0:T(8,128)(2,1)} copy(bf16[128,64,64]{2,1,0:T(8,128)(2,1)S(1)} %gather_fusion.4) | data formatting | bytes 2097152 | tf_op jit(solution)/shard_map/jit(_take)/gather | solution.py:42
  36.8 3.2 %fusion.20 = bf16[16,1,64,64]{2,3,0,1:T(8,128)(2,1)S(1)} fusion(bf16[16,8,64,64]{3,2,1,0:T(8,128)(2,1)} %param.3, bf16[16,8,64,64]{2,3,1,0:T(8,128)(2,1)} %bitcast.68, pred[16,8]{1,0:T(8,128)(4,1)S(1)} %compare_and_fusion, pred[16,8]{1,0:T(8,128)(4,1)S(1)} %fusion.30), kind=kOutput, calls=%fused_computation.17 | convolution fusion | flops 68222976 | bytes 2228480 | tf_op jit(solution)/shard_map/ibxy,iabyz->iaxz/dot_general | solution.py:62
  40.0 0.9 copy.32
  40.9 0.0 all-gather.2.cloned.1.call-update
  40.9 57.6 %all-gather.2.cloned.1.call-done = bf16[16,8,64,64]{3,2,0,1:T(8,128)(2,1)} async-done(((bf16[16,1,64,64]{3,2,0,1:T(8,128)(2,1)}), bf16[16,8,64,64]{3,2,0,1:T(8,128)(2,1)}) %all-gather.2.cloned.1.call-update) | async-done | bytes 1048592 | tf_op jit(solution)/shard_map/all_gather | solution.py:67
  98.5 2.4 %fusion.17 = bf16[16,1,64,64]{2,3,0,1:T(8,128)(2,1)S(1)} fusion(bf16[16,8,64,64]{3,2,0,1:T(8,128)(2,1)} %all-gather.2.cloned.1.call-done, bf16[16,8,64,64]{2,3,1,0:T(8,128)(2,1)S(1)} %bitcast.69, pred[16,8]{1,0:T(8,128)(4,1)S(1)} %compare_and_fusion, pred[16,8]{1,0:T(8,128)(4,1)S(1)} %fusion.30, bf16[16,1,64,64]{2,3,0,1:T(8,128)(2,1)S(1)} %fusion.20), kind=kOutput, calls=%fused_computation.16 | convolution fusion | flops 68485120 | bytes 2359552 | tf_op jit(solution)/shard_map/ibxy,iabyz->iaxz/dot_general | solution.py:65
  100.9 0.9 copy.34
  (16 shorter events, 0.1 us)
Async XLA Ops:
  6.5 8.7 %copy-start = (s32[1536]{0:T(1024)S(1)}, s32[1536]{0:T(1024)}, u32[]{:S(2)}) copy-start(s32[1536]{0:T(1024)} %param.5) | copy-start | bytes 18436
  6.5 8.4 %copy-start.3 = (s32[1536,8]{0,1:T(8,128)S(1)}, s32[1536,8]{0,1:T(8,128)}, u32[]{:S(2)}) copy-start(s32[1536,8]{0,1:T(8,128)} %param.4) | copy-start | bytes 147460
  6.5 91.9 %all-gather.2.cloned.1.call-start = ((), (), s32[]{:S(2)}) async-start(), calls=%async_computation | async-start | bytes 2359296 | tf_op jit(solution)/shard_map/all_gather | solution.py:67
  9.3 16.4 %collective-permute-start = (bf16[8,8,64,64]{3,2,1,0:T(8,128)(2,1)}, bf16[8,8,64,64]{3,2,1,0:T(8,128)(2,1)}, u32[]{:S(2)}, u32[]{:S(2)}) collective-permute-start(bf16[8,8,64,64]{3,2,1,0:T(8,128)(2,1)} %get-tuple-element.23), channel_id=1, source_target_pairs={{0,8},{8,16},{16,24},{24,32},{32,40},{40,48},{48,56},{56,64},{64,7... | collective-permute-start | bytes 1572872 | tf_op jit(solution)/shard_map/ppermute | solution.py:13
  11.2 15.9 %collective-permute-start.1 = (bf16[8,8,64,64]{3,2,1,0:T(8,128)(2,1)S(1)}, bf16[8,8,64,64]{3,2,1,0:T(8,128)(2,1)}, u32[]{:S(2)}, u32[]{:S(2)}) collective-permute-start(bf16[8,8,64,64]{3,2,1,0:T(8,128)(2,1)S(1)} %get-tuple-element.24), channel_id=1, source_target_pairs={{8,0},{16,8},{24,16},{32,24},{40,32},{48,40},{56,48},{64,56},{72,6... | collective-permute-start | bytes 1572872 | tf_op jit(solution)/shard_map/ppermute | solution.py:16
  17.3 9.8 %copy-start.1 = (bf16[16,8,64,64]{3,2,1,0:T(8,128)(2,1)S(1)}, bf16[16,8,64,64]{3,2,1,0:T(8,128)(2,1)}, u32[]{:S(2)}) copy-start(bf16[16,8,64,64]{3,2,1,0:T(8,128)(2,1)} %param.3) | copy-start | bytes 3145732
  36.8 61.6 %copy-start.2 = (bf16[128,64,64]{1,2,0:T(8,128)(2,1)S(1)}, bf16[128,64,64]{1,2,0:T(8,128)(2,1)}, u32[]{:S(2)}) copy-start(bf16[128,64,64]{1,2,0:T(8,128)(2,1)} %copy.31) | copy-start | bytes 3145732
Sparse Core Ops, SparseCore 0:
  41.0 57.4 all-gather.1
where the time goes:
time: 109 us
  waiting for transfers between devices  64.7 us (59%)
  local copies, waits for them, and re-layouts  14.3 us (13%)
  between operations  13.5 us (12%)
  starting transfers between devices  5.55 us (5%)
  matrix products  5.55 us (5%)
  other arithmetic  4.93 us (5%)
    all_gather x1, waiting for transfers between devices, local(): lax.all_gather(square, 'rep', axis=1, tiled=True)  57.6 us
    gather x2, local copies, waits for them, and re-layouts, lookup(): jnp.take(values.reshape(-1, block_side, block_side), flat_index, axis=0)  5.95 us
    ppermute x1, waiting for transfers between devices, with_halo(): lax.ppermute(lax.slice_in_dim(block, block.shape[dim] - width, None, axis...  5.69 us
    concatenate x1, other arithmetic, with_halo(): block = jnp.concatenate([low, block, high], axis=dim)  3.7 us
    ppermute x1, starting transfers between devices, with_halo(): lax.ppermute(lax.slice_in_dim(block, 0, width, axis=dim), axis, backward)  3.64 us
    dot_general x1, matrix products, local(): jnp.einsum('ibxy,iabyz->iaxz', block_values, gathered, preferred_element_...  3.16 us
    slice x1, local copies, waits for them, and re-layouts, with_halo(): lax.slice_in_dim(block, block.shape[dim] - width, None, axis=dim)  2.77 us
    dot_general x1, matrix products, local(): jnp.einsum('ibxy,iabyz->iaxz', lax.all_gather(square, 'rep', axis=1, tile...  2.39 us
  transfers between devices with their start and end apart: 3, of which 3 were waited for; matrix products, arithmetic and copies ran while one was open for 5% of the time, Pallas kernels for 0%

commit v1 on v0

v1 whole, which is shorter than its diff:
```python
import functools

import jax
import jax.numpy as jnp
from jax import lax
from jax.experimental import pallas as pl
from jax.experimental.pallas import tpu as pltpu
from jax.sharding import PartitionSpec as P

HALF = 8
WINDOW = 32
ZERO_TILE = WINDOW * 8
TABLE_ROWS = WINDOW + 8


def swapped(tile):
    return pltpu.roll(tile, 64, 1)


def pack_kernel(x_ref, near_ref, far_ref):
    core = lax.rem(lax.axis_index("rows"), 2)
    for ref, base in ((near_ref, core * HALF), (far_ref, (1 - core) * HALF)):
        for row in range(HALF):
            for pair in range(4):
                ref[row, pair, :, 0:64] = x_ref[base + row, 2 * pair]
                ref[row, pair, :, 64:128] = x_ref[base + row, 2 * pair + 1]


def table_kernel(cols_ref, counts_ref, out_ref):
    total = cols_ref.shape[1]
    chunks = total // 128
    start = lax.rem(lax.axis_index("rows") * (2 * HALF) + (total - HALF), total)
    first = lax.div(start, 128)
    second = lax.rem(first + 1, chunks)
    offset = lax.rem(start, 128)
    shift = lax.rem(256 - offset, 256)

    def window(get):
        both = jnp.concatenate([get(first), get(second)], axis=1)
        return pltpu.roll(both, shift, 1)[:, :128]

    cols = window(lambda k: cols_ref[:, pl.ds(pl.multiple_of(k * 128, 128), 128)])
    counts = window(lambda k: jnp.broadcast_to(counts_ref[pl.ds(k, 1), :], (8, 128)))
    relative = cols - start
    relative = jnp.where(relative < 0, relative + total, relative)
    slot = lax.broadcasted_iota(jnp.int32, (8, 128), 0)
    lane = lax.broadcasted_iota(jnp.int32, (8, 128), 1)
    live = (slot < counts) & (lane < WINDOW)
    matchable = jnp.where(live & (relative < WINDOW), relative, -1)
    column = lax.broadcasted_iota(jnp.int32, (TABLE_ROWS, 128), 0)
    row = lax.broadcasted_iota(jnp.int32, (TABLE_ROWS, 128), 1)
    tiles = jnp.full((TABLE_ROWS, 128), ZERO_TILE, jnp.int32)
    for s in range(8):
        here = jnp.broadcast_to(matchable[s : s + 1, :], (TABLE_ROWS, 128)) == column
        tiles = jnp.where(here, row * 8 + ((s % 2) * 4 + s // 2), tiles)
    out_ref[0:TABLE_ROWS, :] = tiles
    out_ref[TABLE_ROWS : TABLE_ROWS + 8, :] = jnp.where(live, relative, WINDOW)


def half_kernel(far_half, table_ref, center_ref, other_ref, halo_ref, *refs):
    out_ref, store = refs[-2], refs[-1]
    core = lax.rem(lax.axis_index("rows"), 2)
    mine = lax.axis_index("rep")
    low_halo = core if far_half else 1 - core
    center = 2 - low_halo
    swap = lax.rem(mine, 2)
    pair_of = lax.div(mine, 2)

    zeros = jnp.zeros((64, 128), jnp.bfloat16)
    store[ZERO_TILE] = zeros
    store[ZERO_TILE + 4] = zeros
    for ref, chunk in ((center_ref, center), (other_ref, 3 - center), (halo_ref, 3 * (1 - low_halo))):
        for row in range(HALF):
            base = (chunk * HALF + row) * 8
            for pair in range(4):
                tile = ref[row, pair]
                store[base + pair] = tile
                store[base + 4 + pair] = swapped(tile)

    left = lax.broadcasted_iota(jnp.int32, (64, 128), 1) < 64
    for i in range(HALF):
        at = center * HALF + i
        cols = [table_ref[(TABLE_ROWS + (mine ^ q)) * 128 + at] for q in range(8)]
        x = jnp.concatenate([store[at * 8 + swap * 4 + (pair_of ^ p)] for p in range(4)], axis=1)

        def tile(p, b):
            one = table_ref[cols[2 * p] * 128 + cols[b]]
            two = table_ref[cols[2 * p + 1] * 128 + cols[b]] ^ 4
            return jnp.where(left, store[one], store[two])

        squares = []
        for n in range(2):
            total = None
            for k in range(2):
                g = jnp.concatenate(
                    [
                        jnp.concatenate([tile(2 * n + j, 4 * k + b) for j in range(2)], axis=1)
                        for b in range(4)
                    ],
                    axis=0,
                )
                part = jnp.dot(x[:, k * 256 : (k + 1) * 256], g, preferred_element_type=jnp.float32)
                total = part if total is None else total + part
            squares.append(total.astype(jnp.bfloat16))
        cube = None
        for k in range(2):
            g = jnp.concatenate(
                [store[table_ref[cols[0] * 128 + cols[4 * k + b]]] for b in range(4)], axis=0
            )
            part = jnp.dot(squares[k], g, preferred_element_type=jnp.float32)
            cube = part if cube is None else cube + part
        purified = 3.0 * squares[0][:, :128].astype(jnp.float32) - 2.0 * cube
        out_ref[i, 0] = purified[:, :64].astype(jnp.bfloat16)


def vmem():
    return pl.BlockSpec(memory_space=pltpu.VMEM)


def half(far_half, table, center, other, halo, carried, rows_here):
    def out_block():
        core = lax.rem(lax.axis_index("rows"), 2)
        return ((1 - core) if far_half else core, 0, 0, 0)

    shape = jax.ShapeDtypeStruct((rows_here, 1, 64, 64), jnp.bfloat16)
    extra = [] if carried is None else [carried]
    return pl.pallas_call(
        functools.partial(half_kernel, far_half),
        grid=(1,),
        out_shape=shape,
        in_specs=[pl.BlockSpec(memory_space=pltpu.SMEM)]
        + [vmem()] * 3
        + [pl.BlockSpec(memory_space=pl.ANY)] * len(extra),
        out_specs=pl.BlockSpec((HALF, 1, 64, 64), lambda _: out_block()),
        scratch_shapes=[pltpu.VMEM((ZERO_TILE + 8, 64, 128), jnp.bfloat16)],
        input_output_aliases={4: 0} if extra else {},
        compiler_params=pltpu.CompilerParams(vmem_limit_bytes=32 * 1024 * 1024),
        cost_estimate=pl.CostEstimate(flops=600_000_000, bytes_accessed=2_000_000, transcendentals=0),
        name="far_half" if far_half else "near_half",
    )(table, center, other, halo, *extra)


def local(block_values, pattern_cols, pattern_counts):
    rows_here = block_values.shape[0]
    count = lax.axis_size("rows")
    to_core = [(i, i ^ 1) for i in range(count)]
    to_chip = [(i, (i + 1 if i % 2 else i - 1) % count) for i in range(count)]
    packed = jax.ShapeDtypeStruct((HALF, 4, 64, 128), jnp.bfloat16)
    near, far = pl.pallas_call(
        pack_kernel,
        out_shape=(packed, packed),
        in_specs=[vmem()],
        out_specs=(vmem(), vmem()),
        compiler_params=pltpu.CompilerParams(vmem_limit_bytes=32 * 1024 * 1024),
        name="pack",
    )(block_values)
    near_halo = lax.ppermute(near, "rows", to_chip)
    far_halo = lax.ppermute(far, "rows", to_core)
    table = pl.pallas_call(
        table_kernel,
        out_shape=jax.ShapeDtypeStruct((TABLE_ROWS + 8, 128), jnp.int32),
        in_specs=[vmem(), vmem()],
        out_specs=vmem(),
        name="table",
    )(pattern_cols.T, pattern_counts.reshape(-1, 128)).reshape(-1)
    result = half(True, table, far, near, far_halo, None, rows_here)
    return half(False, table, near, far, near_halo, result, rows_here)


def solution(mesh):
    in_specs = (P("rows", None, None, None), P(), P())
    out_specs = P("rows", "rep", None, None)
    return jax.shard_map(local, mesh=mesh, in_specs=in_specs, out_specs=out_specs, check_vma=False)
```

time: 109 us -> 32.7 us (0.30)
  the two profiles are of different devices: /device:TPU:2 before, /device:TPU:56 now
where the time goes in v1:
time: 32.7 us; the launch traced here: 32.4 us
  starting transfers between devices  18.8 us (57%)
  Pallas kernels  11.2 us (34%)
  local copies, waits for them, and re-layouts  2.33 us (7%)
    ppermute x1, starting transfers between devices, local(): near_halo = lax.ppermute(near, 'rows', to_chip)  16.9 us
    pallas_call x2, Pallas kernels, half(): pl.pallas_call(functools.partial(half_kernel, far_half), grid=(1,), out_s...  9.09 us
    unnamed x4, local copies, waits for them, and re-layouts  2.33 us
    ppermute x1, starting transfers between devices, local(): far_halo = lax.ppermute(far, 'rows', to_core)  1.92 us
    pallas_call x1, Pallas kernels, local(): pl.pallas_call(table_kernel, out_shape=jax.ShapeDtypeStruct((TABLE_ROWS +...  1.51 us
  transfers between devices with their start and end apart: 2, of which 0 were waited for; matrix products, arithmetic and copies ran while one was open for 0% of the time, Pallas kernels for 19%

profile of v1, /device:TPU:56, one launch (start us, length us, event | category | flops | bytes accessed | tf_op | source)
XLA Modules:
  0.0 32.4 jit_solution(9233034877673582218)
XLA Ops:
  0.0 0.0 copy-start
  0.0 1.6 %copy-done = bf16[16,8,64,64]{3,2,1,0:T(8,128)(2,1)S(1)} copy-done((bf16[16,8,64,64]{3,2,1,0:T(8,128)(2,1)S(1)}, bf16[16,8,64,64]{3,2,1,0:T(8,128)(2,1)}, u32[]{:S(2)}) %copy-start) | copy-done | bytes 1048600
  1.6 0.6 %pack.1 = (bf16[8,4,64,128]{3,2,1,0:T(8,128)(2,1)S(1)}, bf16[8,4,64,128]{3,2,1,0:T(8,128)(2,1)S(1)}) custom-call(bf16[16,8,64,64]{3,2,1,0:T(8,128)(2,1)S(1)} %copy-done), custom_call_target="tpu_custom_call" | custom-call | tf_op jit(solution)/shard_map/pack/pallas_call | solution.py:149
  2.2 1.9 %collective-permute-start.1 = (bf16[8,4,64,128]{3,2,1,0:T(8,128)(2,1)S(1)}, bf16[8,4,64,128]{3,2,1,0:T(8,128)(2,1)S(1)}, u32[]{:S(2)}, u32[]{:S(2)}) collective-permute-start(bf16[8,4,64,128]{3,2,1,0:T(8,128)(2,1)S(1)} %get-tuple-element.8.center_ref.other_ref), channel_id=1, source_target_pairs={{0,8},{8,0},{16,24},{24,16},{32,40},{40,32},{48,56},{56,48},{64,72... | collective-permute-start | bytes 1572872 | tf_op jit(solution)/shard_map/ppermute | solution.py:158
  4.2 16.9 %collective-permute-start = (bf16[8,4,64,128]{3,2,1,0:T(8,128)(2,1)S(1)}, bf16[8,4,64,128]{3,2,1,0:T(8,128)(2,1)S(1)}, u32[]{:S(2)}, u32[]{:S(2)}) collective-permute-start(bf16[8,4,64,128]{3,2,1,0:T(8,128)(2,1)S(1)} %get-tuple-element.7.other_ref.center_ref), channel_id=1, source_target_pairs={{0,760},{8,16},{16,8},{24,32},{32,24},{40,48},{48,40},{56,64},{64,... | collective-permute-start | bytes 1572872 | tf_op jit(solution)/shard_map/ppermute | solution.py:157
  21.1 1.5 %table.1 = s32[48,128]{1,0:T(8,128)} custom-call(s32[8,1536]{1,0:T(8,128)} %bitcast.5, s32[12,128]{1,0:T(8,128)} %bitcast.6), custom_call_target="tpu_custom_call" | custom-call | tf_op jit(solution)/shard_map/table/pallas_call | solution.py:159
  22.6 0.0 collective-permute-done.1.halo_ref
  22.6 0.0 copy-start.1
  22.6 0.7 %copy-done.1 = s32[48,128]{1,0:T(8,128)S(1)} copy-done((s32[48,128]{1,0:T(8,128)S(1)}, s32[48,128]{1,0:T(8,128)}, u32[]{:S(2)}) %copy-start.1) | copy-done | bytes 24600
  23.3 4.6 %far_half.1.refs_0_ = bf16[16,1,64,64]{3,2,1,0:T(8,128)(2,1)} custom-call(s32[6144]{0:T(1024)S(1)} %bitcast.3, bf16[8,4,64,128]{3,2,1,0:T(8,128)(2,1)S(1)} %get-tuple-element.8.center_ref.other_ref, bf16[8,4,64,128]{3,2,1,0:T(8,128)(2,1)S(1)} %get-tuple-element.7.other_ref.center_ref, bf16[8,4,64,128]{3,2,1,0:T(8,128)(2,1)S(1)} %collective-permute-done.1.halo_ref), custom_call_target="tpu_custom_call" | custom-call | flops 600000000 | bytes 2000000 | tf_op jit(solution)/shard_map/far_half/pallas_call | solution.py:127
  27.9 0.0 collective-permute-done.halo_ref
  27.9 4.5 %near_half.1 = bf16[16,1,64,64]{3,2,1,0:T(8,128)(2,1)} custom-call(s32[6144]{0:T(1024)S(1)} %bitcast.4, bf16[8,4,64,128]{3,2,1,0:T(8,128)(2,1)S(1)} %get-tuple-element.7.other_ref.center_ref, bf16[8,4,64,128]{3,2,1,0:T(8,128)(2,1)S(1)} %get-tuple-element.8.center_ref.other_ref, ...), custom_call_target="tpu_custom_call", output_to_operand_aliasing={{}: (4, {})} | custom-call | flops 600000000 | bytes 2000000 | tf_op jit(solution)/shard_map/near_half/pallas_call | solution.py:127
Async XLA Ops:
  0.0 1.6 %copy-start = (bf16[16,8,64,64]{3,2,1,0:T(8,128)(2,1)S(1)}, bf16[16,8,64,64]{3,2,1,0:T(8,128)(2,1)}, u32[]{:S(2)}) copy-start(bf16[16,8,64,64]{3,2,1,0:T(8,128)(2,1)} %x_ref.1) | copy-start | bytes 3145732
  2.2 20.3 %collective-permute-start.1 = (bf16[8,4,64,128]{3,2,1,0:T(8,128)(2,1)S(1)}, bf16[8,4,64,128]{3,2,1,0:T(8,128)(2,1)S(1)}, u32[]{:S(2)}, u32[]{:S(2)}) collective-permute-start(bf16[8,4,64,128]{3,2,1,0:T(8,128)(2,1)S(1)} %get-tuple-element.8.center_ref.other_ref), channel_id=1, source_target_pairs={{0,8},{8,0},{16,24},{24,16},{32,40},{40,32},{48,56},{56,48},{64,72... | collective-permute-start | bytes 1572872 | tf_op jit(solution)/shard_map/ppermute | solution.py:158
  4.2 23.7 %collective-permute-start = (bf16[8,4,64,128]{3,2,1,0:T(8,128)(2,1)S(1)}, bf16[8,4,64,128]{3,2,1,0:T(8,128)(2,1)S(1)}, u32[]{:S(2)}, u32[]{:S(2)}) collective-permute-start(bf16[8,4,64,128]{3,2,1,0:T(8,128)(2,1)S(1)} %get-tuple-element.7.other_ref.center_ref), channel_id=1, source_target_pairs={{0,760},{8,16},{16,8},{24,32},{32,24},{40,48},{48,40},{56,64},{64,... | collective-permute-start | bytes 1572872 | tf_op jit(solution)/shard_map/ppermute | solution.py:157
  22.6 0.7 %copy-start.1 = (s32[48,128]{1,0:T(8,128)S(1)}, s32[48,128]{1,0:T(8,128)}, u32[]{:S(2)}) copy-start(s32[48,128]{1,0:T(8,128)} %table.1) | copy-start | bytes 73732

commit v2 on v1

--- a/solution.py
+++ b/solution.py
@@ -11,22 +11,42 @@
 WINDOW = 32
 ZERO_TILE = WINDOW * 8
 TABLE_ROWS = WINDOW + 8
+TILE = 64
+PAD = 16
 
 
 def swapped(tile):
     return pltpu.roll(tile, 64, 1)
 
 
-def pack_kernel(x_ref, near_ref, far_ref):
+def pack_half(base, x_ref, out_ref, rows, sems):
+    copies = [
+        pltpu.make_async_copy(x_ref.at[base + row], rows.at[row], sems.at[row])
+        for row in range(HALF)
+    ]
+    for copy in copies:
+        copy.start()
+    for row in range(HALF):
+        copies[row].wait()
+        for pair in range(4):
+            at = pl.ds((row * 4 + pair) * TILE, TILE)
+            out_ref[at, 0:64] = rows[row, 2 * pair]
+            out_ref[at, 64:128] = rows[row, 2 * pair + 1]
+
+
+def near_kernel(x_ref, out_ref, rows, sems):
     core = lax.rem(lax.axis_index("rows"), 2)
-    for ref, base in ((near_ref, core * HALF), (far_ref, (1 - core) * HALF)):
-        for row in range(HALF):
-            for pair in range(4):
-                ref[row, pair, :, 0:64] = x_ref[base + row, 2 * pair]
-                ref[row, pair, :, 64:128] = x_ref[base + row, 2 * pair + 1]
-
-
-def table_kernel(cols_ref, counts_ref, out_ref):
+    out_ref[HALF * 4 * TILE :, :] = jnp.zeros((PAD, 128), jnp.bfloat16)
+    pack_half(core * HALF, x_ref, out_ref, rows, sems)
+
+
+def far_kernel(x_ref, cols_ref, counts_ref, _, out_ref, table_ref, rows, sems):
+    core = lax.rem(lax.axis_index("rows"), 2)
+    make_table(cols_ref, counts_ref, table_ref)
+    pack_half((1 - core) * HALF, x_ref, out_ref, rows, sems)
+
+
+def make_table(cols_ref, counts_ref, out_ref):
     total = cols_ref.shape[1]
     chunks = total // 128
     start = lax.rem(lax.axis_index("rows") * (2 * HALF) + (total - HALF), total)
@@ -57,8 +77,10 @@
     out_ref[TABLE_ROWS : TABLE_ROWS + 8, :] = jnp.where(live, relative, WINDOW)
 
 
-def half_kernel(far_half, table_ref, center_ref, other_ref, halo_ref, *refs):
-    out_ref, store = refs[-2], refs[-1]
+def half_kernel(far_half, table_in, center_ref, other_ref, halo_ref, *refs):
+    out_ref, store, table_ref, squares_ref, sem = refs[-5:]
+    fetch = pltpu.make_async_copy(table_in, table_ref, sem)
+    fetch.start()
     core = lax.rem(lax.axis_index("rows"), 2)
     mine = lax.axis_index("rep")
     low_halo = core if far_half else 1 - core
@@ -73,22 +95,25 @@
         for row in range(HALF):
             base = (chunk * HALF + row) * 8
             for pair in range(4):
-                tile = ref[row, pair]
+                tile = ref[pl.ds((row * 4 + pair) * TILE, TILE), :]
                 store[base + pair] = tile
                 store[base + 4 + pair] = swapped(tile)
-
-    left = lax.broadcasted_iota(jnp.int32, (64, 128), 1) < 64
+    fetch.wait()
+
+    left = lax.broadcasted_iota(jnp.int16, (64, 128), 1) < 64
+    columns = [
+        [table_ref[TABLE_ROWS + (mine ^ q), center * HALF + i] for q in range(8)] for i in range(HALF)
+    ]
     for i in range(HALF):
-        at = center * HALF + i
-        cols = [table_ref[(TABLE_ROWS + (mine ^ q)) * 128 + at] for q in range(8)]
-        x = jnp.concatenate([store[at * 8 + swap * 4 + (pair_of ^ p)] for p in range(4)], axis=1)
+        cols = columns[i]
+        at = (center * HALF + i) * 8 + swap * 4
+        x = jnp.concatenate([store[at + (pair_of ^ p)] for p in range(4)], axis=1)
 
         def tile(p, b):
-            one = table_ref[cols[2 * p] * 128 + cols[b]]
-            two = table_ref[cols[2 * p + 1] * 128 + cols[b]] ^ 4
+            one = table_ref[cols[2 * p], cols[b]]
+            two = table_ref[cols[2 * p + 1], cols[b]] ^ 4
             return jnp.where(left, store[one], store[two])
 
-        squares = []
         for n in range(2):
             total = None
             for k in range(2):
@@ -101,15 +126,17 @@
                 )
                 part = jnp.dot(x[:, k * 256 : (k + 1) * 256], g, preferred_element_type=jnp.float32)
                 total = part if total is None else total + part
-            squares.append(total.astype(jnp.bfloat16))
+            squares_ref[i, :, n * 256 : (n + 1) * 256] = total.astype(jnp.bfloat16)
+    for i in range(HALF):
+        cols = columns[i]
         cube = None
         for k in range(2):
-            g = jnp.concatenate(
-                [store[table_ref[cols[0] * 128 + cols[4 * k + b]]] for b in range(4)], axis=0
+            g = jnp.concatenate([store[table_ref[cols[0], cols[4 * k + b]]] for b in range(4)], axis=0)
+            part = jnp.dot(
+                squares_ref[i, :, k * 256 : (k + 1) * 256], g, preferred_element_type=jnp.float32
             )
-            part = jnp.dot(squares[k], g, preferred_element_type=jnp.float32)
             cube = part if cube is None else cube + part
-        purified = 3.0 * squares[0][:, :128].astype(jnp.float32) - 2.0 * cube
+        purified = 3.0 * squares_ref[i, :, 0:128].astype(jnp.float32) - 2.0 * cube
         out_ref[i, 0] = purified[:, :64].astype(jnp.bfloat16)
 
 
@@ -128,14 +155,18 @@
         functools.partial(half_kernel, far_half),
         grid=(1,),
         out_shape=shape,
-        in_specs=[pl.BlockSpec(memory_space=pltpu.SMEM)]
-        + [vmem()] * 3
+        in_specs=[vmem()] * 4
         + [pl.BlockSpec(memory_space=pl.ANY)] * len(extra),
         out_specs=pl.BlockSpec((HALF, 1, 64, 64), lambda _: out_block()),
-        scratch_shapes=[pltpu.VMEM((ZERO_TILE + 8, 64, 128), jnp.bfloat16)],
+        scratch_shapes=[
+            pltpu.VMEM((ZERO_TILE + 8, 64, 128), jnp.bfloat16),
+            pltpu.SMEM((TABLE_ROWS + 8, 128), jnp.int32),
+            pltpu.VMEM((HALF, 64, 512), jnp.bfloat16),
+            pltpu.SemaphoreType.DMA,
+        ],
         input_output_aliases={4: 0} if extra else {},
         compiler_params=pltpu.CompilerParams(vmem_limit_bytes=32 * 1024 * 1024),
-        cost_estimate=pl.CostEstimate(flops=600_000_000, bytes_accessed=2_000_000, transcendentals=0),
+        cost_estimate=pl.CostEstimate(flops=0, bytes_accessed=0, transcendentals=0),
         name="far_half" if far_half else "near_half",
     )(table, center, other, halo, *extra)
 
@@ -145,24 +176,34 @@
     count = lax.axis_size("rows")
     to_core = [(i, i ^ 1) for i in range(count)]
     to_chip = [(i, (i + 1 if i % 2 else i - 1) % count) for i in range(count)]
-    packed = jax.ShapeDtypeStruct((HALF, 4, 64, 128), jnp.bfloat16)
-    near, far = pl.pallas_call(
-        pack_kernel,
-        out_shape=(packed, packed),
-        in_specs=[vmem()],
-        out_specs=(vmem(), vmem()),
-        compiler_params=pltpu.CompilerParams(vmem_limit_bytes=32 * 1024 * 1024),
-        name="pack",
+    packed = [jax.ShapeDtypeStruct((HALF * 4 * TILE + pad, 128), jnp.bfloat16) for pad in (PAD, 0)]
+    block_values = pltpu.with_memory_space_constraint(block_values, pltpu.HBM)
+    hbm = pl.BlockSpec(memory_space=pltpu.HBM)
+    scratch = [pltpu.VMEM((HALF, 8, 64, 64), jnp.bfloat16), pltpu.SemaphoreType.DMA((HALF,))]
+    free = pl.CostEstimate(flops=0, bytes_accessed=0, transcendentals=0)
+    params = pltpu.CompilerParams(vmem_limit_bytes=32 * 1024 * 1024)
+    near = pl.pallas_call(
+        near_kernel,
+        out_shape=packed[0],
+        in_specs=[hbm],
+        out_specs=vmem(),
+        scratch_shapes=scratch,
+        compiler_params=params,
+        cost_estimate=free,
+        name="pack_near",
     )(block_values)
     near_halo = lax.ppermute(near, "rows", to_chip)
+    far, table = pl.pallas_call(
+        far_kernel,
+        out_shape=(packed[1], jax.ShapeDtypeStruct((TABLE_ROWS + 8, 128), jnp.int32)),
+        in_specs=[hbm, vmem(), vmem(), pl.BlockSpec(memory_space=pl.ANY)],
+        out_specs=(vmem(), vmem()),
+        scratch_shapes=scratch,
+        compiler_params=params,
+        cost_estimate=free,
+        name="pack_far",
+    )(block_values, pattern_cols.T, pattern_counts.reshape(-1, 128), near)
     far_halo = lax.ppermute(far, "rows", to_core)
-    table = pl.pallas_call(
-        table_kernel,
-        out_shape=jax.ShapeDtypeStruct((TABLE_ROWS + 8, 128), jnp.int32),
-        in_specs=[vmem(), vmem()],
-        out_specs=vmem(),
-        name="table",
-    )(pattern_cols.T, pattern_counts.reshape(-1, 128)).reshape(-1)
     result = half(True, table, far, near, far_halo, None, rows_here)
     return half(False, table, near, far, near_halo, result, rows_here)
 

time: 32.7 us -> 31.6 us (0.966)
  the two profiles are of different devices: /device:TPU:56 before, /device:TPU:1 now
where the time goes in v2:
time: 31.6 us; the launch traced here: 31.4 us
  starting transfers between devices  19.6 us (62%)
  Pallas kernels  10.2 us (32%)
  waiting for transfers between devices  1.52 us (5%)
    ppermute x1, starting transfers between devices, local(): far_halo = lax.ppermute(far, 'rows', to_core)  15.1 us
    pallas_call x2, Pallas kernels, half(): pl.pallas_call(functools.partial(half_kernel, far_half), grid=(1,), out_s...  6.58 us
    ppermute x1, starting transfers between devices, local(): near_halo = lax.ppermute(near, 'rows', to_chip)  4.51 us
    pallas_call x1, Pallas kernels, local(): pl.pallas_call(near_kernel, out_shape=packed[0], in_specs=[hbm], out_spec...  1.82 us
    pallas_call x1, Pallas kernels, local(): pl.pallas_call(far_kernel, out_shape=(packed[1], jax.ShapeDtypeStruct((TA...  1.8 us
    ppermute x1, waiting for transfers between devices, local(): far_halo = lax.ppermute(far, 'rows', to_core)  1.51 us
  transfers between devices with their start and end apart: 2, of which 1 were waited for; matrix products, arithmetic and copies ran while one was open for 0% of the time, Pallas kernels for 16%

profile of v2, /device:TPU:1, one launch (start us, length us, event | category | flops | bytes accessed | tf_op | source)
XLA Modules:
  0.0 31.4 jit_solution(3215934711821605823)
XLA Ops:
  0.0 0.0 copy-start
  0.0 0.0 copy-start.1
  0.0 1.8 %pack_near.1._.other_ref.center_ref = bf16[2064,128]{1,0:T(8,128)(2,1)S(1)} custom-call(bf16[16,8,64,64]{3,2,1,0:T(8,128)(2,1)} %x_ref.3), custom_call_target="tpu_custom_call" | custom-call | tf_op jit(solution)/shard_map/pack_near/pallas_call | solution.py:185
  1.8 4.5 %collective-permute-start = (bf16[2064,128]{1,0:T(8,128)(2,1)S(1)}, bf16[2064,128]{1,0:T(8,128)(2,1)S(1)}, u32[]{:S(2)}, u32[]{:S(2)}) collective-permute-start(bf16[2064,128]{1,0:T(8,128)(2,1)S(1)} %pack_near.1._.other_ref.center_ref), channel_id=1, source_target_pairs={{0,760},{8,16},{16,8},{24,32},{32,24},{40,48},{48,40},{56,64},{64,... | collective-permute-start | bytes 1585160 | tf_op jit(solution)/shard_map/ppermute | solution.py:195
  6.3 0.0 copy-done
  6.4 0.0 copy-done.1
  6.4 1.8 %pack_far.1 = (bf16[2048,128]{1,0:T(8,128)(2,1)S(1)}, s32[48,128]{1,0:T(8,128)S(1)}) custom-call(bf16[16,8,64,64]{3,2,1,0:T(8,128)(2,1)} %x_ref.3, s32[8,1536]{1,0:T(8,128)S(1)} %bitcast.2, s32[12,128]{1,0:T(8,128)S(1)} %bitcast.3, bf16[2064,128]{1,0:T(8,128)(2,1)S(1)} %pack_near.1._.other_ref.center_ref), custom_call_target="tpu_custom_call" | custom-call | tf_op jit(solution)/shard_map/pack_far/pallas_call | solution.py:196
  8.2 15.1 %collective-permute-start.1 = (bf16[2048,128]{1,0:T(8,128)(2,1)S(1)}, bf16[2048,128]{1,0:T(8,128)(2,1)S(1)}, u32[]{:S(2)}, u32[]{:S(2)}) collective-permute-start(bf16[2048,128]{1,0:T(8,128)(2,1)S(1)} %get-tuple-element.8.center_ref.other_ref), channel_id=1, source_target_pairs={{0,8},{8,0},{16,24},{24,16},{32,40},{40,32},{48,56},{56,48},{64,72... | collective-permute-start | bytes 1572872 | tf_op jit(solution)/shard_map/ppermute | solution.py:206
  23.3 1.5 %collective-permute-done.1.halo_ref = bf16[2048,128]{1,0:T(8,128)(2,1)S(1)} collective-permute-done((bf16[2048,128]{1,0:T(8,128)(2,1)S(1)}, bf16[2048,128]{1,0:T(8,128)(2,1)S(1)}, u32[]{:S(2)}, u32[]{:S(2)}) %collective-permute-start.1) | collective-permute-done | bytes 524320 | tf_op jit(solution)/shard_map/ppermute | solution.py:206
  24.8 3.3 %far_half.1.refs_0_ = bf16[16,1,64,64]{3,2,1,0:T(8,128)(2,1)} custom-call(s32[48,128]{1,0:T(8,128)S(1)} %get-tuple-element.7.table_in, bf16[2048,128]{1,0:T(8,128)(2,1)S(1)} %get-tuple-element.8.center_ref.other_ref, bf16[2064,128]{1,0:T(8,128)(2,1)S(1)} %pack_near.1._.other_ref.center_ref, bf16[2048,128]{1,0:T(8,128)(2,1)S(1)} %collective-permute-done.1.halo_ref), custom_call_target="tpu_custom_call" | custom-call | tf_op jit(solution)/shard_map/far_half/pallas_call | solution.py:154
  28.1 0.0 collective-permute-done.halo_ref
  28.1 3.3 %near_half.1 = bf16[16,1,64,64]{3,2,1,0:T(8,128)(2,1)} custom-call(s32[48,128]{1,0:T(8,128)S(1)} %get-tuple-element.7.table_in, bf16[2064,128]{1,0:T(8,128)(2,1)S(1)} %pack_near.1._.other_ref.center_ref, bf16[2048,128]{1,0:T(8,128)(2,1)S(1)} %get-tuple-element.8.center_ref.other_ref, ...), custom_call_target="tpu_custom_call", output_to_operand_aliasing={{}: (4, {})} | custom-call | tf_op jit(solution)/shard_map/near_half/pallas_call | solution.py:154
Async XLA Ops:
  0.0 6.3 %copy-start = (s32[1536,8]{0,1:T(8,128)S(1)}, s32[1536,8]{0,1:T(8,128)}, u32[]{:S(2)}) copy-start(s32[1536,8]{0,1:T(8,128)} %param.4) | copy-start | bytes 147460
  0.0 6.4 %copy-start.1 = (s32[1536]{0:T(1024)S(1)}, s32[1536]{0:T(1024)}, u32[]{:S(2)}) copy-start(s32[1536]{0:T(1024)} %param.5) | copy-start | bytes 18436
  1.8 26.3 %collective-permute-start = (bf16[2064,128]{1,0:T(8,128)(2,1)S(1)}, bf16[2064,128]{1,0:T(8,128)(2,1)S(1)}, u32[]{:S(2)}, u32[]{:S(2)}) collective-permute-start(bf16[2064,128]{1,0:T(8,128)(2,1)S(1)} %pack_near.1._.other_ref.center_ref), channel_id=1, source_target_pairs={{0,760},{8,16},{16,8},{24,32},{32,24},{40,48},{48,40},{56,64},{64,... | collective-permute-start | bytes 1585160 | tf_op jit(solution)/shard_map/ppermute | solution.py:195
  8.2 16.6 %collective-permute-start.1 = (bf16[2048,128]{1,0:T(8,128)(2,1)S(1)}, bf16[2048,128]{1,0:T(8,128)(2,1)S(1)}, u32[]{:S(2)}, u32[]{:S(2)}) collective-permute-start(bf16[2048,128]{1,0:T(8,128)(2,1)S(1)} %get-tuple-element.8.center_ref.other_ref), channel_id=1, source_target_pairs={{0,8},{8,0},{16,24},{24,16},{32,40},{40,32},{48,56},{56,48},{64,72... | collective-permute-start | bytes 1572872 | tf_op jit(solution)/shard_map/ppermute | solution.py:206

commit v3 on v2

--- a/solution.py
+++ b/solution.py
@@ -8,6 +8,7 @@
 from jax.sharding import PartitionSpec as P
 
 HALF = 8
+PIECE = 4
 WINDOW = 32
 ZERO_TILE = WINDOW * 8
 TABLE_ROWS = WINDOW + 8
@@ -19,34 +20,27 @@
     return pltpu.roll(tile, 64, 1)
 
 
-def pack_half(base, x_ref, out_ref, rows, sems):
+def pack_kernel(x_ref, near_ref, far_ref, rows, sems):
+    core = lax.rem(lax.axis_index("rows"), 2)
+    starts = (core * HALF, core * HALF + PIECE, (1 - core) * HALF, (1 - core) * HALF + PIECE)
     copies = [
-        pltpu.make_async_copy(x_ref.at[base + row], rows.at[row], sems.at[row])
-        for row in range(HALF)
+        pltpu.make_async_copy(x_ref.at[pl.ds(start, PIECE)], rows.at[pl.ds(n * PIECE, PIECE)], sems.at[n])
+        for n, start in enumerate(starts)
     ]
     for copy in copies:
         copy.start()
-    for row in range(HALF):
-        copies[row].wait()
-        for pair in range(4):
-            at = pl.ds((row * 4 + pair) * TILE, TILE)
-            out_ref[at, 0:64] = rows[row, 2 * pair]
-            out_ref[at, 64:128] = rows[row, 2 * pair + 1]
-
-
-def near_kernel(x_ref, out_ref, rows, sems):
-    core = lax.rem(lax.axis_index("rows"), 2)
-    out_ref[HALF * 4 * TILE :, :] = jnp.zeros((PAD, 128), jnp.bfloat16)
-    pack_half(core * HALF, x_ref, out_ref, rows, sems)
-
-
-def far_kernel(x_ref, cols_ref, counts_ref, _, out_ref, table_ref, rows, sems):
-    core = lax.rem(lax.axis_index("rows"), 2)
-    make_table(cols_ref, counts_ref, table_ref)
-    pack_half((1 - core) * HALF, x_ref, out_ref, rows, sems)
-
-
-def make_table(cols_ref, counts_ref, out_ref):
+    near_ref[HALF * 4 * TILE :, :] = jnp.zeros((PAD, 128), jnp.bfloat16)
+    for n, copy in enumerate(copies):
+        copy.wait()
+        out_ref = far_ref if n // 2 else near_ref
+        for row in range(PIECE):
+            for pair in range(4):
+                at = pl.ds((((n % 2) * PIECE + row) * 4 + pair) * TILE, TILE)
+                blocks = [rows[n * PIECE + row, 2 * pair + side] for side in range(2)]
+                out_ref[at, :] = jnp.concatenate(blocks, axis=1)
+
+
+def table_kernel(cols_ref, counts_ref, out_ref):
     total = cols_ref.shape[1]
     chunks = total // 128
     start = lax.rem(lax.axis_index("rows") * (2 * HALF) + (total - HALF), total)
@@ -178,32 +172,30 @@
     to_chip = [(i, (i + 1 if i % 2 else i - 1) % count) for i in range(count)]
     packed = [jax.ShapeDtypeStruct((HALF * 4 * TILE + pad, 128), jnp.bfloat16) for pad in (PAD, 0)]
     block_values = pltpu.with_memory_space_constraint(block_values, pltpu.HBM)
-    hbm = pl.BlockSpec(memory_space=pltpu.HBM)
-    scratch = [pltpu.VMEM((HALF, 8, 64, 64), jnp.bfloat16), pltpu.SemaphoreType.DMA((HALF,))]
     free = pl.CostEstimate(flops=0, bytes_accessed=0, transcendentals=0)
-    params = pltpu.CompilerParams(vmem_limit_bytes=32 * 1024 * 1024)
-    near = pl.pallas_call(
-        near_kernel,
-        out_shape=packed[0],
-        in_specs=[hbm],
-        out_specs=vmem(),
-        scratch_shapes=scratch,
-        compiler_params=params,
+    near, far = pl.pallas_call(
+        pack_kernel,
+        out_shape=packed,
+        in_specs=[pl.BlockSpec(memory_space=pltpu.HBM)],
+        out_specs=[vmem(), vmem()],
+        scratch_shapes=[
+            pltpu.VMEM((2 * HALF, 8, 64, 64), jnp.bfloat16),
+            pltpu.SemaphoreType.DMA((2 * HALF // PIECE,)),
+        ],
+        compiler_params=pltpu.CompilerParams(vmem_limit_bytes=32 * 1024 * 1024),
         cost_estimate=free,
-        name="pack_near",
+        name="pack",
     )(block_values)
     near_halo = lax.ppermute(near, "rows", to_chip)
-    far, table = pl.pallas_call(
-        far_kernel,
-        out_shape=(packed[1], jax.ShapeDtypeStruct((TABLE_ROWS + 8, 128), jnp.int32)),
-        in_specs=[hbm, vmem(), vmem(), pl.BlockSpec(memory_space=pl.ANY)],
-        out_specs=(vmem(), vmem()),
-        scratch_shapes=scratch,
-        compiler_params=params,
+    far_halo = lax.ppermute(far, "rows", to_core)
+    table = pl.pallas_call(
+        table_kernel,
+        out_shape=jax.ShapeDtypeStruct((TABLE_ROWS + 8, 128), jnp.int32),
+        in_specs=[vmem(), vmem()],
+        out_specs=vmem(),
         cost_estimate=free,
-        name="pack_far",
-    )(block_values, pattern_cols.T, pattern_counts.reshape(-1, 128), near)
-    far_halo = lax.ppermute(far, "rows", to_core)
+        name="table",
+    )(pattern_cols.T, pattern_counts.reshape(-1, 128))
     result = half(True, table, far, near, far_halo, None, rows_here)
     return half(False, table, near, far, near_halo, result, rows_here)
 

time: 31.6 us -> 30.5 us (0.965)
  waiting for transfers between devices: 1.52 us -> 0.01 us
  local copies, waits for them, and re-layouts: 0.01 us -> 0.74 us
  Pallas kernels: 10.2 us -> 9.77 us
    ppermute x1, waiting for transfers between devices: 1.51 us -> 0.01 us  [local(): far_halo = lax.ppermute(far, 'rows', to_core)]
    unnamed x4 -> x2, local copies, waits for them, and re-layouts: 0.01 us -> 0.74 us
    pallas_call x2, Pallas kernels: 3.62 us -> 3.19 us  [the longest x1 1.68 us: local(): pl.pallas_call(pack_kernel, out_shape=packed, in_specs=[pl.BlockSpec(memo...]
  transfers between devices with their start and end apart: 2 -> 2, of which waited for: 1 -> 0; matrix products, arithmetic and copies ran while one was open for 0% -> 0% of each run, Pallas kernels for 16% -> 16%
where the time goes in v3:
time: 30.5 us; the launch traced here: 30.2 us
  starting transfers between devices  19.6 us (64%)
  Pallas kernels  9.77 us (32%)
  local copies, waits for them, and re-layouts  0.74 us (2%)
    ppermute x1, starting transfers between devices, local(): far_halo = lax.ppermute(far, 'rows', to_core)  15.1 us
    pallas_call x2, Pallas kernels, half(): pl.pallas_call(functools.partial(half_kernel, far_half), grid=(1,), out_s...  6.58 us
    ppermute x1, starting transfers between devices, local(): near_halo = lax.ppermute(near, 'rows', to_chip)  4.51 us
    pallas_call x1, Pallas kernels, local(): pl.pallas_call(pack_kernel, out_shape=packed, in_specs=[pl.BlockSpec(memo...  1.68 us
    pallas_call x1, Pallas kernels, local(): pl.pallas_call(table_kernel, out_shape=jax.ShapeDtypeStruct((TABLE_ROWS +...  1.51 us
    unnamed x2, local copies, waits for them, and re-layouts  0.74 us
  transfers between devices with their start and end apart: 2, of which 0 were waited for; matrix products, arithmetic and copies ran while one was open for 0% of the time, Pallas kernels for 16%

profile of v3, /device:TPU:1, one launch (start us, length us, event | category | flops | bytes accessed | tf_op | source)
XLA Modules:
  0.0 30.2 jit_solution(2452972984694848040)
XLA Ops:
  0.0 1.7 %pack.1 = (bf16[2064,128]{1,0:T(8,128)(2,1)S(1)}, bf16[2048,128]{1,0:T(8,128)(2,1)S(1)}) custom-call(bf16[16,8,64,64]{3,2,1,0:T(8,128)(2,1)} %x_ref.1), custom_call_target="tpu_custom_call" | custom-call | tf_op jit(solution)/shard_map/pack/pallas_call | solution.py:176
  1.7 4.5 %collective-permute-start = (bf16[2064,128]{1,0:T(8,128)(2,1)S(1)}, bf16[2064,128]{1,0:T(8,128)(2,1)S(1)}, u32[]{:S(2)}, u32[]{:S(2)}) collective-permute-start(bf16[2064,128]{1,0:T(8,128)(2,1)S(1)} %get-tuple-element.7.other_ref.center_ref), channel_id=1, source_target_pairs={{0,760},{8,16},{16,8},{24,32},{32,24},{40,48},{48,40},{56,64},{64,... | collective-permute-start | bytes 1585160 | tf_op jit(solution)/shard_map/ppermute | solution.py:189
  6.2 15.1 %collective-permute-start.1 = (bf16[2048,128]{1,0:T(8,128)(2,1)S(1)}, bf16[2048,128]{1,0:T(8,128)(2,1)S(1)}, u32[]{:S(2)}, u32[]{:S(2)}) collective-permute-start(bf16[2048,128]{1,0:T(8,128)(2,1)S(1)} %get-tuple-element.8.center_ref.other_ref), channel_id=1, source_target_pairs={{0,8},{8,0},{16,24},{24,16},{32,40},{40,32},{48,56},{56,48},{64,72... | collective-permute-start | bytes 1572872 | tf_op jit(solution)/shard_map/ppermute | solution.py:190
  21.3 1.5 %table.1.table_in = s32[48,128]{1,0:T(8,128)} custom-call(s32[8,1536]{1,0:T(8,128)} %bitcast.2, s32[12,128]{1,0:T(8,128)} %bitcast.3), custom_call_target="tpu_custom_call" | custom-call | tf_op jit(solution)/shard_map/table/pallas_call | solution.py:191
  22.8 0.0 collective-permute-done.1.halo_ref
  22.9 0.0 copy-start
  22.9 0.7 %copy-done = s32[48,128]{1,0:T(8,128)S(1)} copy-done((s32[48,128]{1,0:T(8,128)S(1)}, s32[48,128]{1,0:T(8,128)}, u32[]{:S(2)}) %copy-start) | copy-done | bytes 24600
  23.6 3.3 %far_half.1.refs_0_ = bf16[16,1,64,64]{3,2,1,0:T(8,128)(2,1)} custom-call(s32[48,128]{1,0:T(8,128)S(1)} %copy-done, bf16[2048,128]{1,0:T(8,128)(2,1)S(1)} %get-tuple-element.8.center_ref.other_ref, bf16[2064,128]{1,0:T(8,128)(2,1)S(1)} %get-tuple-element.7.other_ref.center_ref, bf16[2048,128]{1,0:T(8,128)(2,1)S(1)} %collective-permute-done.1.halo_ref), custom_call_target="tpu_custom_call" | custom-call | tf_op jit(solution)/shard_map/far_half/pallas_call | solution.py:148
  26.9 0.0 collective-permute-done.halo_ref
  26.9 3.3 %near_half.1 = bf16[16,1,64,64]{3,2,1,0:T(8,128)(2,1)} custom-call(s32[48,128]{1,0:T(8,128)S(1)} %copy-done, bf16[2064,128]{1,0:T(8,128)(2,1)S(1)} %get-tuple-element.7.other_ref.center_ref, bf16[2048,128]{1,0:T(8,128)(2,1)S(1)} %get-tuple-element.8.center_ref.other_ref, ...), custom_call_target="tpu_custom_call", output_to_operand_aliasing={{}: (4, {})} | custom-call | tf_op jit(solution)/shard_map/near_half/pallas_call | solution.py:148
Async XLA Ops:
  1.7 25.2 %collective-permute-start = (bf16[2064,128]{1,0:T(8,128)(2,1)S(1)}, bf16[2064,128]{1,0:T(8,128)(2,1)S(1)}, u32[]{:S(2)}, u32[]{:S(2)}) collective-permute-start(bf16[2064,128]{1,0:T(8,128)(2,1)S(1)} %get-tuple-element.7.other_ref.center_ref), channel_id=1, source_target_pairs={{0,760},{8,16},{16,8},{24,32},{32,24},{40,48},{48,40},{56,64},{64,... | collective-permute-start | bytes 1585160 | tf_op jit(solution)/shard_map/ppermute | solution.py:189
  6.2 16.6 %collective-permute-start.1 = (bf16[2048,128]{1,0:T(8,128)(2,1)S(1)}, bf16[2048,128]{1,0:T(8,128)(2,1)S(1)}, u32[]{:S(2)}, u32[]{:S(2)}) collective-permute-start(bf16[2048,128]{1,0:T(8,128)(2,1)S(1)} %get-tuple-element.8.center_ref.other_ref), channel_id=1, source_target_pairs={{0,8},{8,0},{16,24},{24,16},{32,40},{40,32},{48,56},{56,48},{64,72... | collective-permute-start | bytes 1572872 | tf_op jit(solution)/shard_map/ppermute | solution.py:190
  22.9 0.7 %copy-start = (s32[48,128]{1,0:T(8,128)S(1)}, s32[48,128]{1,0:T(8,128)}, u32[]{:S(2)}) copy-start(s32[48,128]{1,0:T(8,128)} %table.1.table_in) | copy-start | bytes 73732

commit v4 on v3

v4 whole, which is shorter than its diff:
```python
import jax
import jax.numpy as jnp
from jax import lax
from jax.experimental import pallas as pl
from jax.experimental.pallas import tpu as pltpu
from jax.sharding import PartitionSpec as P

HALF = 8
PIECE = 4
WINDOW = 32
TILE = 64
PAD = 16
GROUP = 12
ZERO_TILE = WINDOW * GROUP
STORE = (ZERO_TILE + 8, TILE, 128)
STRIDE = 64
TABLE = (24, 128)
COLUMNS = WINDOW * STRIDE + STRIDE


def fill(store, chunk, ref):
    for row in range(HALF):
        base = (chunk * HALF + row) * GROUP
        for pair in range(4):
            tile = ref[pl.ds((row * 4 + pair) * TILE, TILE), :]
            store[base + pair] = tile
            store[base + 4 + pair] = pltpu.roll(tile, 64, 1)
            store[base + 8 + pair] = tile


def pack_kernel(x_ref, near_ref, far_ref, rows, sems):
    core = lax.rem(lax.axis_index("rows"), 2)
    starts = (core * HALF, core * HALF + PIECE, (1 - core) * HALF, (1 - core) * HALF + PIECE)
    copies = [
        pltpu.make_async_copy(x_ref.at[pl.ds(start, PIECE)], rows.at[pl.ds(n * PIECE, PIECE)], sems.at[n])
        for n, start in enumerate(starts)
    ]
    for copy in copies:
        copy.start()
    near_ref[HALF * 4 * TILE :, :] = jnp.zeros((PAD, 128), jnp.bfloat16)
    for n, copy in enumerate(copies):
        copy.wait()
        out_ref = far_ref if n // 2 else near_ref
        for row in range(PIECE):
            for pair in range(4):
                at = pl.ds((((n % 2) * PIECE + row) * 4 + pair) * TILE, TILE)
                blocks = [rows[n * PIECE + row, 2 * pair + side] for side in range(2)]
                out_ref[at, :] = jnp.concatenate(blocks, axis=1)


def own_kernel(near_ref, far_ref, cols_in, counts_in, table_ref, store, cols_ref, counts_ref, sems):
    copies = [
        pltpu.make_async_copy(cols_in, cols_ref, sems.at[0]),
        pltpu.make_async_copy(counts_in, counts_ref, sems.at[1]),
    ]
    for copy in copies:
        copy.start()
    core = lax.rem(lax.axis_index("rows"), 2)
    zeros = jnp.zeros((TILE, 128), jnp.bfloat16)
    store[ZERO_TILE] = zeros
    store[ZERO_TILE + 4] = zeros
    fill(store, 1 + core, near_ref)
    fill(store, 2 - core, far_ref)
    for copy in copies:
        copy.wait()
    total = cols_ref.shape[1]
    chunks = total // 128
    start = lax.rem(lax.axis_index("rows") * (2 * HALF) + (total - HALF), total)
    first = lax.div(start, 128)
    second = lax.rem(first + 1, chunks)
    shift = lax.rem(256 - lax.rem(start, 128), 256)

    def window(get):
        both = jnp.concatenate([get(first), get(second)], axis=1)
        return pltpu.roll(both, shift, 1)[:, :128]

    cols = window(lambda k: cols_ref[:, pl.ds(pl.multiple_of(k * 128, 128), 128)])
    counts = window(lambda k: jnp.broadcast_to(counts_ref[pl.ds(k, 1), :], (8, 128)))
    relative = cols - start
    relative = jnp.where(relative < 0, relative + total, relative)
    slot = lax.broadcasted_iota(jnp.int32, (8, 128), 0)
    lane = lax.broadcasted_iota(jnp.int32, (8, 128), 1)
    live = (slot < counts) & (lane < WINDOW)
    matchable = jnp.where(live & (relative < WINDOW), relative, -1)
    matchable = jnp.where(lane < STRIDE, matchable, pltpu.roll(matchable, STRIDE, 1))
    line = lax.broadcasted_iota(jnp.int32, (16, 128), 0)
    lane = lax.broadcasted_iota(jnp.int32, (16, 128), 1)
    column = line * 2 + lane // STRIDE
    row = lane % STRIDE
    tiles = jnp.full((16, 128), ZERO_TILE, jnp.int32)
    for s in range(8):
        here = jnp.broadcast_to(matchable[s : s + 1, :], (16, 128)) == column
        tiles = jnp.where(here, row * GROUP + ((s % 2) * 4 + s // 2), tiles)
    table_ref[0:16, :] = tiles
    columns = pltpu.roll(jnp.where(live, relative, WINDOW), STRIDE, 1)
    table_ref[16:24, :] = jnp.where(lane[0:8, :] < STRIDE, ZERO_TILE, columns)


def purify(table_in, halo_ref, store, table_ref, squares_ref, sem, center, halo_chunk, put):
    fetch = pltpu.make_async_copy(table_in, table_ref, sem)
    fetch.start()
    mine = lax.axis_index("rep")
    swap = lax.rem(mine, 2)
    pair_of = lax.div(mine, 2)
    fill(store, halo_chunk, halo_ref)
    left = lax.broadcasted_iota(jnp.int16, (TILE, 128), 1) < 64
    fetch.wait()
    rows = [
        [table_ref[COLUMNS + (mine ^ q) * 128 + center * HALF + i] for q in range(8)]
        for i in range(HALF)
    ]
    for i in range(HALF):
        cols = [c * STRIDE for c in rows[i]]
        at = (center * HALF + i) * GROUP + swap * 4
        x = jnp.concatenate([store[at + (pair_of ^ p)] for p in range(4)], axis=1)

        def tile(p, b):
            one = table_ref[cols[2 * p] + rows[i][b]]
            two = table_ref[cols[2 * p + 1] + rows[i][b]]
            return jnp.where(left, store[one], store[two + 4])

        for n in range(2):
            total = None
            for k in range(2):
                g = jnp.concatenate(
                    [
                        jnp.concatenate([tile(2 * n + j, 4 * k + b) for j in range(2)], axis=1)
                        for b in range(4)
                    ],
                    axis=0,
                )
                part = jnp.dot(x[:, k * 256 : (k + 1) * 256], g, preferred_element_type=jnp.float32)
                total = part if total is None else total + part
            squares_ref[i, :, n * 256 : (n + 1) * 256] = total.astype(jnp.bfloat16)
    for i in range(HALF):
        column = rows[i][0] * STRIDE
        cube = None
        for k in range(2):
            g = jnp.concatenate([store[table_ref[column + rows[i][4 * k + b]]] for b in range(4)], axis=0)
            part = jnp.dot(
                squares_ref[i, :, k * 256 : (k + 1) * 256], g, preferred_element_type=jnp.float32
            )
            cube = part if cube is None else cube + part
        purified = 3.0 * squares_ref[i, :, 0:128].astype(jnp.float32) - 2.0 * cube
        put(i, purified[:, :64].astype(jnp.bfloat16))


def far_kernel(table_in, halo_ref, _, out_ref, store, table_ref, squares_ref, sem):
    core = lax.rem(lax.axis_index("rows"), 2)

    def put(i, block):
        out_ref[i] = block

    purify(table_in, halo_ref, store, table_ref, squares_ref, sem, 2 - core, 3 * (1 - core), put)


def near_kernel(table_in, halo_ref, far_ref, _, out_ref, store, table_ref, squares_ref, sem, near, sems):
    core = lax.rem(lax.axis_index("rows"), 2)
    far_out = pltpu.make_async_copy(far_ref, out_ref.at[pl.ds((1 - core) * HALF, HALF), 0], sems.at[0])
    far_out.start()

    def put(i, block):
        near[i] = block

    purify(table_in, halo_ref, store, table_ref, squares_ref, sem, 1 + core, 3 * core, put)
    near_out = pltpu.make_async_copy(near, out_ref.at[pl.ds(core * HALF, HALF), 0], sems.at[1])
    near_out.start()
    far_out.wait()
    near_out.wait()


def vmem():
    return pl.BlockSpec(memory_space=pltpu.VMEM)


def hbm():
    return pl.BlockSpec(memory_space=pltpu.HBM)


def call(kernel, name, args, in_specs, out_shape, out_specs, scratch_shapes=(), aliases=None):
    return pl.pallas_call(
        kernel,
        out_shape=out_shape,
        in_specs=in_specs,
        out_specs=out_specs,
        scratch_shapes=scratch_shapes,
        input_output_aliases=aliases or {},
        compiler_params=pltpu.CompilerParams(vmem_limit_bytes=16 * 1024 * 1024),
        cost_estimate=pl.CostEstimate(flops=0, bytes_accessed=0, transcendentals=0),
        name=name,
    )(*args)


def local(block_values, pattern_cols, pattern_counts):
    count = lax.axis_size("rows")
    to_core = [(i, i ^ 1) for i in range(count)]
    to_chip = [(i, (i + 1 if i % 2 else i - 1) % count) for i in range(count)]
    bf16, i32 = jnp.bfloat16, jnp.int32
    near, far = call(
        pack_kernel,
        "pack",
        [pltpu.with_memory_space_constraint(block_values, pltpu.HBM)],
        [hbm()],
        [jax.ShapeDtypeStruct((HALF * 4 * TILE + pad, 128), bf16) for pad in (PAD, 0)],
        [vmem(), vmem()],
        [
            pltpu.VMEM((2 * HALF, 8, 64, 64), bf16),
            pltpu.SemaphoreType.DMA((2 * HALF // PIECE,)),
        ],
    )
    near_halo = lax.ppermute(near, "rows", to_chip)
    far_halo = lax.ppermute(far, "rows", to_core)
    cols, counts = pattern_cols.T, pattern_counts.reshape(-1, 128)
    stored = jax.ShapeDtypeStruct(STORE, bf16)
    table, store = call(
        own_kernel,
        "own",
        [near, far, *(pltpu.with_memory_space_constraint(x, pltpu.HBM) for x in (cols, counts))],
        [vmem(), vmem(), hbm(), hbm()],
        [jax.ShapeDtypeStruct(TABLE, i32), stored],
        [vmem(), vmem()],
        [
            pltpu.VMEM(cols.shape, i32),
            pltpu.VMEM(counts.shape, i32),
            pltpu.SemaphoreType.DMA((2,)),
        ],
    )
    table = table.reshape(-1)
    scratch = [
        pltpu.SMEM((TABLE[0] * TABLE[1],), i32),
        pltpu.VMEM((HALF, 64, 512), bf16),
        pltpu.SemaphoreType.DMA,
    ]
    far_result, store = call(
        far_kernel,
        "far_half",
        [table, far_halo, store],
        [vmem()] * 3,
        [jax.ShapeDtypeStruct((HALF, 64, 64), bf16), stored],
        [vmem(), vmem()],
        scratch,
        {2: 1},
    )
    result, _ = call(
        near_kernel,
        "near_half",
        [table, near_halo, far_result, store],
        [vmem()] * 4,
        [jax.ShapeDtypeStruct((2 * HALF, 1, 64, 64), bf16), stored],
        [hbm(), vmem()],
        scratch + [pltpu.VMEM((HALF, 64, 64), bf16), pltpu.SemaphoreType.DMA((2,))],
        {3: 1},
    )
    return result


def solution(mesh):
    in_specs = (P("rows", None, None, None), P(), P())
    out_specs = P("rows", "rep", None, None)
    return jax.shard_map(local, mesh=mesh, in_specs=in_specs, out_specs=out_specs, check_vma=False)
```

time: 30.5 us -> 27.9 us (0.915)
  Pallas kernels: 9.77 us -> 7.86 us
  local copies, waits for them, and re-layouts: 0.74 us -> 0 us
    pallas_call x4, Pallas kernels: 9.77 us -> 7.86 us  [call(): pl.pallas_call(kernel, out_shape=out_shape, in_specs=in_specs, out_specs=...]
    unnamed x2 -> x0, local copies, waits for them, and re-layouts: 0.74 us -> none
  transfers between devices with their start and end apart: 2 -> 2, of which waited for: 0 -> 1; matrix products, arithmetic and copies ran while one was open for 0% -> 0% of each run, Pallas kernels for 16% -> 12%
where the time goes in v4:
time: 27.9 us; the launch traced here: 27.6 us
  starting transfers between devices  19.6 us (70%)
  Pallas kernels  7.86 us (28%)
    ppermute x1, starting transfers between devices, local(): far_halo = lax.ppermute(far, 'rows', to_core)  15.1 us
    pallas_call x4, Pallas kernels, call(): pl.pallas_call(kernel, out_shape=out_shape, in_specs=in_specs, out_specs=...  7.86 us
    ppermute x1, starting transfers between devices, local(): near_halo = lax.ppermute(near, 'rows', to_chip)  4.51 us
  transfers between devices with their start and end apart: 2, of which 1 were waited for; matrix products, arithmetic and copies ran while one was open for 0% of the time, Pallas kernels for 12%

profile of v4, /device:TPU:1, one launch (start us, length us, event | category | flops | bytes accessed | tf_op | source)
XLA Modules:
  0.0 27.6 jit_solution(5963222423898012442)
XLA Ops:
  0.0 1.7 %pack.1 = (bf16[2064,128]{1,0:T(8,128)(2,1)S(1)}, bf16[2048,128]{1,0:T(8,128)(2,1)S(1)}) custom-call(bf16[16,8,64,64]{3,2,1,0:T(8,128)(2,1)} %x_ref.1), custom_call_target="tpu_custom_call" | custom-call | tf_op jit(solution)/shard_map/pack/pallas_call | solution.py:181
  1.7 4.5 %collective-permute-start = (bf16[2064,128]{1,0:T(8,128)(2,1)S(1)}, bf16[2064,128]{1,0:T(8,128)(2,1)S(1)}, u32[]{:S(2)}, u32[]{:S(2)}) collective-permute-start(bf16[2064,128]{1,0:T(8,128)(2,1)S(1)} %get-tuple-element.12.near_ref), channel_id=1, source_target_pairs={{0,760},{8,16},{16,8},{24,32},{32,24},{40,48},{48,40},{56,64},{64,... | collective-permute-start | bytes 1585160 | tf_op jit(solution)/shard_map/ppermute | solution.py:211
  6.2 15.1 %collective-permute-start.1 = (bf16[2048,128]{1,0:T(8,128)(2,1)S(1)}, bf16[2048,128]{1,0:T(8,128)(2,1)S(1)}, u32[]{:S(2)}, u32[]{:S(2)}) collective-permute-start(bf16[2048,128]{1,0:T(8,128)(2,1)S(1)} %get-tuple-element.13.far_ref), channel_id=1, source_target_pairs={{0,8},{8,0},{16,24},{24,16},{32,40},{40,32},{48,56},{56,48},{64,72... | collective-permute-start | bytes 1572872 | tf_op jit(solution)/shard_map/ppermute | solution.py:212
  21.3 1.4 %own.1 = (s32[24,128]{1,0:T(8,128)S(1)}, bf16[392,64,128]{2,1,0:T(8,128)(2,1)S(1)}) custom-call(bf16[2064,128]{1,0:T(8,128)(2,1)S(1)} %get-tuple-element.12.near_ref, bf16[2048,128]{1,0:T(8,128)(2,1)S(1)} %get-tuple-element.13.far_ref, s32[8,1536]{1,0:T(8,128)} %bitcast.5, s32[12,128]{1,0:T(8,128)} %bitcast.6), custom_call_target="tpu_custom_call" | custom-call | tf_op jit(solution)/shard_map/own/pallas_call | solution.py:181
  22.8 0.1 collective-permute-done.1.halo_ref
  22.9 2.0 %far_half.1 = (bf16[8,64,64]{2,1,0:T(8,128)(2,1)S(1)}, bf16[392,64,128]{2,1,0:T(8,128)(2,1)S(1)}) custom-call(s32[3072]{0:T(1024)S(1)} %bitcast.3, bf16[2048,128]{1,0:T(8,128)(2,1)S(1)} %collective-permute-done.1.halo_ref, bf16[392,64,128]{2,1,0:T(8,128)(2,1)S(1)} %get-tuple-element.15._), custom_call_target="tpu_custom_call", output_to_operand_aliasing={{1}: (2, {})} | custom-call | tf_op jit(solution)/shard_map/far_half/pallas_call | solution.py:181
  24.9 0.0 collective-permute-done.halo_ref
  24.9 2.7 %near_half.1 = (bf16[16,1,64,64]{3,2,1,0:T(8,128)(2,1)}, bf16[392,64,128]{2,1,0:T(8,128)(2,1)S(1)}) custom-call(s32[3072]{0:T(1024)S(1)} %bitcast.4, bf16[2064,128]{1,0:T(8,128)(2,1)S(1)} %collective-permute-done.halo_ref, bf16[8,64,64]{2,1,0:T(8,128)(2,1)S(1)} %get-tuple-element.16.far_ref, ...), custom_call_target="tpu_custom_call", output_to_operand_aliasing={{1}: (3, {})} | custom-call | tf_op jit(solution)/shard_map/near_half/pallas_call | solution.py:181
Async XLA Ops:
  1.7 23.2 %collective-permute-start = (bf16[2064,128]{1,0:T(8,128)(2,1)S(1)}, bf16[2064,128]{1,0:T(8,128)(2,1)S(1)}, u32[]{:S(2)}, u32[]{:S(2)}) collective-permute-start(bf16[2064,128]{1,0:T(8,128)(2,1)S(1)} %get-tuple-element.12.near_ref), channel_id=1, source_target_pairs={{0,760},{8,16},{16,8},{24,32},{32,24},{40,48},{48,40},{56,64},{64,... | collective-permute-start | bytes 1585160 | tf_op jit(solution)/shard_map/ppermute | solution.py:211
  6.2 16.6 %collective-permute-start.1 = (bf16[2048,128]{1,0:T(8,128)(2,1)S(1)}, bf16[2048,128]{1,0:T(8,128)(2,1)S(1)}, u32[]{:S(2)}, u32[]{:S(2)}) collective-permute-start(bf16[2048,128]{1,0:T(8,128)(2,1)S(1)} %get-tuple-element.13.far_ref), channel_id=1, source_target_pairs={{0,8},{8,0},{16,24},{24,16},{32,40},{40,32},{48,56},{56,48},{64,72... | collective-permute-start | bytes 1572872 | tf_op jit(solution)/shard_map/ppermute | solution.py:212

commit v5 on v4

--- a/solution.py
+++ b/solution.py
@@ -28,24 +28,55 @@
             store[base + 8 + pair] = tile
 
 
-def pack_kernel(x_ref, near_ref, far_ref, rows, sems):
-    core = lax.rem(lax.axis_index("rows"), 2)
-    starts = (core * HALF, core * HALF + PIECE, (1 - core) * HALF, (1 - core) * HALF + PIECE)
-    copies = [
+def from_pieces(x_ref, rows, sems, starts):
+    return [
         pltpu.make_async_copy(x_ref.at[pl.ds(start, PIECE)], rows.at[pl.ds(n * PIECE, PIECE)], sems.at[n])
         for n, start in enumerate(starts)
     ]
-    for copy in copies:
-        copy.start()
-    near_ref[HALF * 4 * TILE :, :] = jnp.zeros((PAD, 128), jnp.bfloat16)
+
+
+def pack(copies, rows, out_ref):
     for n, copy in enumerate(copies):
         copy.wait()
-        out_ref = far_ref if n // 2 else near_ref
-        for row in range(PIECE):
+        for row in range(n * PIECE, (n + 1) * PIECE):
             for pair in range(4):
-                at = pl.ds((((n % 2) * PIECE + row) * 4 + pair) * TILE, TILE)
-                blocks = [rows[n * PIECE + row, 2 * pair + side] for side in range(2)]
+                at = pl.ds((row * 4 + pair) * TILE, TILE)
+                blocks = [rows[row, 2 * pair + side] for side in range(2)]
                 out_ref[at, :] = jnp.concatenate(blocks, axis=1)
+
+
+def pack_kernel(x_ref, near_ref, far_ref, near_rows, far_rows, near_sems, far_sems):
+    me = lax.axis_index("rows")
+    core = lax.rem(me, 2)
+    late = me == lax.axis_size("rows") - 1
+    near = from_pieces(x_ref, near_rows, near_sems, (core * HALF, core * HALF + PIECE))
+    far = from_pieces(x_ref, far_rows, far_sems, ((1 - core) * HALF, (1 - core) * HALF + PIECE))
+    for copy in near:
+        copy.start()
+
+    @pl.when(jnp.logical_not(late))
+    def _():
+        for copy in far:
+            copy.start()
+
+    near_ref[HALF * 4 * TILE :, :] = jnp.zeros((PAD, 128), jnp.bfloat16)
+    pack(near, near_rows, near_ref)
+
+    @pl.when(jnp.logical_not(late))
+    def _():
+        pack(far, far_rows, far_ref)
+
+
+def rest_kernel(x_ref, _, far_ref, far_rows, far_sems):
+    me = lax.axis_index("rows")
+    core = lax.rem(me, 2)
+
+    @pl.when(me == lax.axis_size("rows") - 1)
+    def _():
+        far = from_pieces(x_ref, far_rows, far_sems, ((1 - core) * HALF, (1 - core) * HALF + PIECE))
+        for copy in far:
+            copy.start()
+        pack(far, far_rows, far_ref)
 
 
 def own_kernel(near_ref, far_ref, cols_in, counts_in, table_ref, store, cols_ref, counts_ref, sems):
@@ -96,15 +127,11 @@
     table_ref[16:24, :] = jnp.where(lane[0:8, :] < STRIDE, ZERO_TILE, columns)
 
 
-def purify(table_in, halo_ref, store, table_ref, squares_ref, sem, center, halo_chunk, put):
-    fetch = pltpu.make_async_copy(table_in, table_ref, sem)
-    fetch.start()
+def purify(table_ref, store, squares_ref, center, put):
     mine = lax.axis_index("rep")
     swap = lax.rem(mine, 2)
     pair_of = lax.div(mine, 2)
-    fill(store, halo_chunk, halo_ref)
     left = lax.broadcasted_iota(jnp.int16, (TILE, 128), 1) < 64
-    fetch.wait()
     rows = [
         [table_ref[COLUMNS + (mine ^ q) * 128 + center * HALF + i] for q in range(8)]
         for i in range(HALF)
@@ -146,26 +173,59 @@
 
 
 def far_kernel(table_in, halo_ref, _, out_ref, store, table_ref, squares_ref, sem):
-    core = lax.rem(lax.axis_index("rows"), 2)
+    me = lax.axis_index("rows")
+    core = lax.rem(me, 2)
+    fetch = pltpu.make_async_copy(table_in, table_ref, sem)
+    fetch.start()
+    fill(store, 3 * (1 - core), halo_ref)
+    fetch.wait()
 
     def put(i, block):
         out_ref[i] = block
 
-    purify(table_in, halo_ref, store, table_ref, squares_ref, sem, 2 - core, 3 * (1 - core), put)
-
-
-def near_kernel(table_in, halo_ref, far_ref, _, out_ref, store, table_ref, squares_ref, sem, near, sems):
-    core = lax.rem(lax.axis_index("rows"), 2)
-    far_out = pltpu.make_async_copy(far_ref, out_ref.at[pl.ds((1 - core) * HALF, HALF), 0], sems.at[0])
-    far_out.start()
+    @pl.when(me != 1)
+    def _():
+        purify(table_ref, store, squares_ref, 2 - core, put)
+
+
+def near_kernel(
+    table_in, halo_ref, far_in, _, out_ref, store, table_ref, squares_ref, sem, near, far, sems
+):
+    me = lax.axis_index("rows")
+    core = lax.rem(me, 2)
+    fetch = pltpu.make_async_copy(table_in, table_ref, sem)
+    fetch.start()
+    near_out = pltpu.make_async_copy(near, out_ref.at[pl.ds(core * HALF, HALF), 0], sems.at[0])
+    far_at = out_ref.at[pl.ds((1 - core) * HALF, HALF), 0]
+    far_out = pltpu.make_async_copy(far_in, far_at, sems.at[1])
+
+    @pl.when(me != 1)
+    def _():
+        far_out.start()
+
+    fill(store, 3 * core, halo_ref)
+    fetch.wait()
 
     def put(i, block):
         near[i] = block
 
-    purify(table_in, halo_ref, store, table_ref, squares_ref, sem, 1 + core, 3 * core, put)
-    near_out = pltpu.make_async_copy(near, out_ref.at[pl.ds(core * HALF, HALF), 0], sems.at[1])
+    purify(table_ref, store, squares_ref, 1 + core, put)
     near_out.start()
-    far_out.wait()
+
+    @pl.when(me == 1)
+    def _():
+        def put_far(i, block):
+            far[i] = block
+
+        purify(table_ref, store, squares_ref, 2 - core, put_far)
+        late_out = pltpu.make_async_copy(far, far_at, sems.at[1])
+        late_out.start()
+        late_out.wait()
+
+    @pl.when(me != 1)
+    def _():
+        far_out.wait()
+
     near_out.wait()
 
 
@@ -196,17 +256,22 @@
     to_core = [(i, i ^ 1) for i in range(count)]
     to_chip = [(i, (i + 1 if i % 2 else i - 1) % count) for i in range(count)]
     bf16, i32 = jnp.bfloat16, jnp.int32
+    block_values = pltpu.with_memory_space_constraint(block_values, pltpu.HBM)
+    rows = [pltpu.VMEM((HALF, 8, 64, 64), bf16)]
+    sems = [pltpu.SemaphoreType.DMA((HALF // PIECE,))]
+    packed = [jax.ShapeDtypeStruct((HALF * 4 * TILE + pad, 128), bf16) for pad in (PAD, 0)]
     near, far = call(
-        pack_kernel,
-        "pack",
-        [pltpu.with_memory_space_constraint(block_values, pltpu.HBM)],
-        [hbm()],
-        [jax.ShapeDtypeStruct((HALF * 4 * TILE + pad, 128), bf16) for pad in (PAD, 0)],
-        [vmem(), vmem()],
-        [
-            pltpu.VMEM((2 * HALF, 8, 64, 64), bf16),
-            pltpu.SemaphoreType.DMA((2 * HALF // PIECE,)),
-        ],
+        pack_kernel, "pack", [block_values], [hbm()], packed, [vmem(), vmem()], rows * 2 + sems * 2
+    )
+    far = call(
+        rest_kernel,
+        "rest",
+        [block_values, far],
+        [hbm(), vmem()],
+        packed[1],
+        vmem(),
+        rows + sems,
+        {1: 0},
     )
     near_halo = lax.ppermute(near, "rows", to_chip)
     far_halo = lax.ppermute(far, "rows", to_core)
@@ -248,7 +313,7 @@
         [vmem()] * 4,
         [jax.ShapeDtypeStruct((2 * HALF, 1, 64, 64), bf16), stored],
         [hbm(), vmem()],
-        scratch + [pltpu.VMEM((HALF, 64, 64), bf16), pltpu.SemaphoreType.DMA((2,))],
+        scratch + [pltpu.VMEM((HALF, 64, 64), bf16)] * 2 + [pltpu.SemaphoreType.DMA((2,))],
         {3: 1},
     )
     return result

time: 27.9 us -> 27.4 us (0.982)
  starting transfers between devices: 19.6 us -> 19.2 us
    ppermute x1, starting transfers between devices: 15.1 us -> 14.7 us  [local(): far_halo = lax.ppermute(far, 'rows', to_core)]
    pallas_call x4 -> x5, Pallas kernels: 7.86 us -> 7.86 us  [call(): pl.pallas_call(kernel, out_shape=out_shape, in_specs=in_specs, out_specs=...]
  transfers between devices with their start and end apart: 2 -> 2, of which waited for: 1 -> 1; matrix products, arithmetic and copies ran while one was open for 0% -> 0% of each run, Pallas kernels for 12% -> 8%
where the time goes in v5:
time: 27.4 us; the launch traced here: 27.2 us
  starting transfers between devices  19.2 us (70%)
  Pallas kernels  7.86 us (29%)
    ppermute x1, starting transfers between devices, local(): far_halo = lax.ppermute(far, 'rows', to_core)  14.7 us
    pallas_call x5, Pallas kernels, call(): pl.pallas_call(kernel, out_shape=out_shape, in_specs=in_specs, out_specs=...  7.86 us
    ppermute x1, starting transfers between devices, local(): near_halo = lax.ppermute(near, 'rows', to_chip)  4.51 us
  transfers between devices with their start and end apart: 2, of which 1 were waited for; matrix products, arithmetic and copies ran while one was open for 0% of the time, Pallas kernels for 8%

profile of v5, /device:TPU:1, one launch (start us, length us, event | category | flops | bytes accessed | tf_op | source)
XLA Modules:
  0.0 27.2 jit_solution(1758834070553070104)
XLA Ops:
  0.0 1.8 %pack.1 = (bf16[2064,128]{1,0:T(8,128)(2,1)S(1)}, bf16[2048,128]{1,0:T(8,128)(2,1)S(1)}) custom-call(bf16[16,8,64,64]{3,2,1,0:T(8,128)(2,1)} %x_ref.3), custom_call_target="tpu_custom_call" | custom-call | tf_op jit(solution)/shard_map/pack/pallas_call | solution.py:241
  1.8 4.5 %collective-permute-start = (bf16[2064,128]{1,0:T(8,128)(2,1)S(1)}, bf16[2064,128]{1,0:T(8,128)(2,1)S(1)}, u32[]{:S(2)}, u32[]{:S(2)}) collective-permute-start(bf16[2064,128]{1,0:T(8,128)(2,1)S(1)} %get-tuple-element.12.near_ref), channel_id=1, source_target_pairs={{0,760},{8,16},{16,8},{24,32},{32,24},{40,48},{48,40},{56,64},{64,... | collective-permute-start | bytes 1585160 | tf_op jit(solution)/shard_map/ppermute | solution.py:276
  6.4 14.7 %collective-permute-start.1 = (bf16[2048,128]{1,0:T(8,128)(2,1)S(1)}, bf16[2048,128]{1,0:T(8,128)(2,1)S(1)}, u32[]{:S(2)}, u32[]{:S(2)}) collective-permute-start(bf16[2048,128]{1,0:T(8,128)(2,1)S(1)} %rest.1.far_ref), channel_id=1, source_target_pairs={{0,8},{8,0},{16,24},{24,16},{32,40},{40,32},{48,56},{56,48},{64,72... | collective-permute-start | bytes 1572872 | tf_op jit(solution)/shard_map/ppermute | solution.py:277
  21.1 1.4 %own.1 = (s32[24,128]{1,0:T(8,128)S(1)}, bf16[392,64,128]{2,1,0:T(8,128)(2,1)S(1)}) custom-call(bf16[2064,128]{1,0:T(8,128)(2,1)S(1)} %get-tuple-element.12.near_ref, bf16[2048,128]{1,0:T(8,128)(2,1)S(1)} %rest.1.far_ref, s32[8,1536]{1,0:T(8,128)} %bitcast.5, s32[12,128]{1,0:T(8,128)} %bitcast.6), custom_call_target="tpu_custom_call" | custom-call | tf_op jit(solution)/shard_map/own/pallas_call | solution.py:241
  22.5 0.1 collective-permute-done.1.halo_ref
  22.6 0.8 %far_half.1 = (bf16[8,64,64]{2,1,0:T(8,128)(2,1)S(1)}, bf16[392,64,128]{2,1,0:T(8,128)(2,1)S(1)}) custom-call(s32[3072]{0:T(1024)S(1)} %bitcast.3, bf16[2048,128]{1,0:T(8,128)(2,1)S(1)} %collective-permute-done.1.halo_ref, bf16[392,64,128]{2,1,0:T(8,128)(2,1)S(1)} %get-tuple-element.15._), custom_call_target="tpu_custom_call", output_to_operand_aliasing={{1}: (2, {})} | custom-call | tf_op jit(solution)/shard_map/far_half/pallas_call | solution.py:241
  23.4 0.0 collective-permute-done.halo_ref
  23.4 3.8 %near_half.1 = (bf16[16,1,64,64]{3,2,1,0:T(8,128)(2,1)}, bf16[392,64,128]{2,1,0:T(8,128)(2,1)S(1)}) custom-call(s32[3072]{0:T(1024)S(1)} %bitcast.4, bf16[2064,128]{1,0:T(8,128)(2,1)S(1)} %collective-permute-done.halo_ref, bf16[8,64,64]{2,1,0:T(8,128)(2,1)S(1)} %get-tuple-element.16.far_in, ...), custom_call_target="tpu_custom_call", output_to_operand_aliasing={{1}: (3, {})} | custom-call | tf_op jit(solution)/shard_map/near_half/pallas_call | solution.py:241
  (1 shorter events, 0.0 us)
Async XLA Ops:
  1.8 21.6 %collective-permute-start = (bf16[2064,128]{1,0:T(8,128)(2,1)S(1)}, bf16[2064,128]{1,0:T(8,128)(2,1)S(1)}, u32[]{:S(2)}, u32[]{:S(2)}) collective-permute-start(bf16[2064,128]{1,0:T(8,128)(2,1)S(1)} %get-tuple-element.12.near_ref), channel_id=1, source_target_pairs={{0,760},{8,16},{16,8},{24,32},{32,24},{40,48},{48,40},{56,64},{64,... | collective-permute-start | bytes 1585160 | tf_op jit(solution)/shard_map/ppermute | solution.py:276
  6.4 16.2 %collective-permute-start.1 = (bf16[2048,128]{1,0:T(8,128)(2,1)S(1)}, bf16[2048,128]{1,0:T(8,128)(2,1)S(1)}, u32[]{:S(2)}, u32[]{:S(2)}) collective-permute-start(bf16[2048,128]{1,0:T(8,128)(2,1)S(1)} %rest.1.far_ref), channel_id=1, source_target_pairs={{0,8},{8,0},{16,24},{24,16},{32,40},{40,32},{48,56},{56,48},{64,72... | collective-permute-start | bytes 1572872 | tf_op jit(solution)/shard_map/ppermute | solution.py:277

commit v6 on v5

v6 whole, which is shorter than its diff:
```python
import functools

import jax
import jax.numpy as jnp
from jax import lax
from jax.experimental import pallas as pl
from jax.experimental.pallas import tpu as pltpu
from jax.sharding import PartitionSpec as P

HALF = 8
PIECE = 4
WINDOW = 32
TILE = 64
PAD = 16
GROUP = 12
ZERO_TILE = WINDOW * GROUP
STORE = (ZERO_TILE + 8, TILE, 128)
TABLES = (2, 8, 128)
DEAD = (WINDOW - 1, 0)
COLUMN_LINE = (6, 1)


def fill(store, chunk, ref):
    for row in range(HALF):
        base = (chunk * HALF + row) * GROUP
        for pair in range(4):
            tile = ref[pl.ds((row * 4 + pair) * TILE, TILE), :]
            store[base + pair] = tile
            store[base + 4 + pair] = pltpu.roll(tile, 64, 1)
            store[base + 8 + pair] = tile


def from_pieces(x_ref, rows, sems, starts):
    return [
        pltpu.make_async_copy(x_ref.at[pl.ds(start, PIECE)], rows.at[pl.ds(n * PIECE, PIECE)], sems.at[n])
        for n, start in enumerate(starts)
    ]


def pack(copies, rows, out_ref):
    for n, copy in enumerate(copies):
        copy.wait()
        for row in range(n * PIECE, (n + 1) * PIECE):
            for pair in range(4):
                at = pl.ds((row * 4 + pair) * TILE, TILE)
                blocks = [rows[row, 2 * pair + side] for side in range(2)]
                out_ref[at, :] = jnp.concatenate(blocks, axis=1)


def rest_kernel(x_ref, _, far_ref, far_rows, far_sems):
    me = lax.axis_index("rows")
    core = lax.rem(me, 2)

    @pl.when(me == lax.axis_size("rows") - 1)
    def _():
        far = from_pieces(x_ref, far_rows, far_sems, ((1 - core) * HALF, (1 - core) * HALF + PIECE))
        for copy in far:
            copy.start()
        pack(far, far_rows, far_ref)


def own(near_ref, far_ref, cols_in, counts_in, table_ref, store, cols_ref, counts_ref, sems):
    copies = [
        pltpu.make_async_copy(cols_in, cols_ref, sems.at[0]),
        pltpu.make_async_copy(counts_in, counts_ref, sems.at[1]),
    ]
    for copy in copies:
        copy.start()
    core = lax.rem(lax.axis_index("rows"), 2)
    zeros = jnp.zeros((TILE, 128), jnp.bfloat16)
    store[ZERO_TILE] = zeros
    store[ZERO_TILE + 4] = zeros
    fill(store, 1 + core, near_ref)
    fill(store, 2 - core, far_ref)
    for copy in copies:
        copy.wait()
    total = cols_ref.shape[1]
    chunks = total // 128
    start = lax.rem(lax.axis_index("rows") * (2 * HALF) + (total - HALF), total)
    first = lax.div(start, 128)
    second = lax.rem(first + 1, chunks)
    shift = lax.rem(256 - lax.rem(start, 128), 256)

    def window(get):
        both = jnp.concatenate([get(first), get(second)], axis=1)
        return pltpu.roll(both, shift, 1)[:, :128]

    cols = window(lambda k: cols_ref[:, pl.ds(pl.multiple_of(k * 128, 128), 128)])
    counts = window(lambda k: jnp.broadcast_to(counts_ref[pl.ds(k, 1), :], (8, 128)))
    relative = cols - start
    relative = jnp.where(relative < 0, relative + total, relative)
    slot = lax.broadcasted_iota(jnp.int32, (8, 128), 0)
    lane = lax.broadcasted_iota(jnp.int32, (8, 128), 1)
    live = (slot < counts) & (lane < WINDOW)
    matchable = jnp.where(live & (relative < WINDOW), relative, -1)
    matchable = functools.reduce(
        jnp.maximum, [matchable] + [pltpu.roll(matchable, by, 1) for by in (32, 64, 96)]
    )
    column = slot * 4 + lane // WINDOW
    row = lane % WINDOW
    tiles = jnp.full((8, 128), ZERO_TILE, jnp.int32)
    for s in range(8):
        here = jnp.broadcast_to(matchable[s : s + 1, :], (8, 128)) == column
        tiles = jnp.where(here, row * GROUP + ((s % 2) * 4 + s // 2), tiles)
    reached = ((column < 24) & (row < 24), (column >= 8) & (row >= 8))
    for high in range(2):
        columns = jnp.where(live, relative, DEAD[high])
        line = jnp.zeros((8, 128), jnp.int32)
        for s in range(8):
            moved = pltpu.roll(columns, (s * 8 - HALF * (1 + high)) % 128, 1)
            line = jnp.where(lane // 8 == s, jnp.broadcast_to(moved[s : s + 1, :], (8, 128)), line)
        words = jnp.where(reached[high], tiles, ZERO_TILE)
        table_ref[high] = jnp.where(slot == COLUMN_LINE[high], line, words)


def columns_of(word, center):
    mine = lax.axis_index("rep")
    start = jnp.where(center == 1, COLUMN_LINE[0], COLUMN_LINE[1]) * 128
    return [
        [word(start + (mine ^ q) * 8 + i) for q in range(8)] for i in range(HALF)
    ]


def left_side():
    return lax.broadcasted_iota(jnp.int16, (TILE, 128), 1) < 64


def gathered(word, store, left, cols, sources, n):
    def tile(p, source):
        one = word(cols[2 * p] * WINDOW + source)
        two = word(cols[2 * p + 1] * WINDOW + source)
        return jnp.where(left, store[one], store[two + 4])

    return jnp.concatenate(
        [jnp.concatenate([tile(2 * n + j, b) for j in range(2)], axis=1) for b in sources], axis=0
    )


def product(x, word, store, left, cols, sources, n):
    total = None
    for k in range(0, len(sources), 4):
        g = gathered(word, store, left, cols, sources[k : k + 4], n)
        part = jnp.dot(x[:, k * 64 : (k + 4) * 64], g, preferred_element_type=jnp.float32)
        total = part if total is None else total + part
    return total


def squares(word, store, center, rows, put, skip=None):
    mine = lax.axis_index("rep")
    left = left_side()
    for i in range(HALF):
        at = (center * HALF + i) * GROUP + lax.rem(mine, 2) * 4
        x = jnp.concatenate([store[at + (lax.div(mine, 2) ^ p)] for p in range(4)], axis=1)
        sources = rows[i]
        if skip is not None:
            sources = [jnp.where(lax.div(c, HALF) == skip, DEAD[0], c) for c in sources]
        for n in range(2):
            put(i, n, product(x, word, store, left, rows[i], sources, n))


def low_halo_squares(word, store, rows, put):
    left = left_side()
    for i in range(HALF):
        sources = list(range(i, HALF + i % 2))
        found = [word(w * WINDOW + HALF + i) if w < HALF else ZERO_TILE for w in sources]
        x = jnp.concatenate(
            [
                jnp.where(left, store[found[k]], store[found[k + 1] + 4])
                for k in range(0, len(sources), 2)
            ],
            axis=1,
        )
        for n in range(2):
            put(i, n, product(x, word, store, left, rows[i], sources, n))


def cubes(word, store, squares_ref, rows, put):
    for i in range(HALF):
        cube = None
        for k in range(2):
            g = jnp.concatenate(
                [store[word(rows[i][0] * WINDOW + c)] for c in rows[i][4 * k : 4 * k + 4]], axis=0
            )
            part = jnp.dot(
                squares_ref[i, :, k * 256 : (k + 1) * 256], g, preferred_element_type=jnp.float32
            )
            cube = part if cube is None else cube + part
        purified = 3.0 * squares_ref[i, :, 0:128].astype(jnp.float32) - 2.0 * cube
        put(i, purified[:, :64].astype(jnp.bfloat16))


def rounded(squares_ref, before=None):
    def put(i, n, total):
        at = slice(n * 256, (n + 1) * 256)
        if before is not None:
            total = total + before[i, :, at]
        squares_ref[i, :, at] = total.astype(jnp.bfloat16)

    return put


def pack_kernel(
    x_ref,
    cols_in,
    counts_in,
    near_ref,
    far_ref,
    tables_ref,
    store,
    early_ref,
    near_rows,
    far_rows,
    near_sems,
    far_sems,
    cols_ref,
    counts_ref,
    own_sems,
    table_ref,
    fetch_sem,
):
    me = lax.axis_index("rows")
    core = lax.rem(me, 2)
    late = me == lax.axis_size("rows") - 1
    near = from_pieces(x_ref, near_rows, near_sems, (core * HALF, core * HALF + PIECE))
    far = from_pieces(x_ref, far_rows, far_sems, ((1 - core) * HALF, (1 - core) * HALF + PIECE))
    for copy in near:
        copy.start()

    @pl.when(jnp.logical_not(late))
    def _():
        for copy in far:
            copy.start()

    near_ref[HALF * 4 * TILE :, :] = jnp.zeros((PAD, 128), jnp.bfloat16)
    pack(near, near_rows, near_ref)

    @pl.when(jnp.logical_not(late))
    def _():
        pack(far, far_rows, far_ref)

    @pl.when(me == 0)
    def _():
        own(near_ref, far_ref, cols_in, counts_in, tables_ref, store, cols_ref, counts_ref, own_sems)
        fetch = pltpu.make_async_copy(tables_ref.at[0], table_ref, fetch_sem)
        fetch.start()
        fetch.wait()

        def word(at):
            return table_ref[lax.div(at, 128), lax.rem(at, 128)]

        def put(i, n, total):
            early_ref[i, :, n * 256 : (n + 1) * 256] = total

        squares(word, store, 1, columns_of(word, 1), put, skip=0)


def own_kernel(near_ref, far_ref, cols_in, counts_in, _, __, tables_ref, store, cols_ref, counts_ref, sems):
    @pl.when(lax.axis_index("rows") != 0)
    def _():
        own(near_ref, far_ref, cols_in, counts_in, tables_ref, store, cols_ref, counts_ref, sems)


def one_table(tables_in, half):
    words = TABLES[1] * TABLES[2]
    return tables_in.at[pl.ds(pl.multiple_of(half * words, words), words)]


def far_kernel(tables_in, halo_ref, _, out_ref, store, table_ref, squares_ref, sems):
    me = lax.axis_index("rows")
    core = lax.rem(me, 2)
    fetch = pltpu.make_async_copy(one_table(tables_in, 1 - core), table_ref, sems.at[0])

    @pl.when(me != 1)
    def _():
        fetch.start()

    fill(store, 3 * (1 - core), halo_ref)

    def put(i, block):
        out_ref[i] = block

    @pl.when(me != 1)
    def _():
        fetch.wait()
        rows = columns_of(table_ref.__getitem__, 2 - core)
        squares(table_ref.__getitem__, store, 2 - core, rows, rounded(squares_ref))
        cubes(table_ref.__getitem__, store, squares_ref, rows, put)


def near_kernel(
    tables_in, halo_ref, far_in, early_ref, _, out_ref, store, table_ref, far_table, squares_ref, sems, near, far
):
    me = lax.axis_index("rows")
    core = lax.rem(me, 2)
    fetch = pltpu.make_async_copy(one_table(tables_in, core), table_ref, sems.at[0])
    fetch.start()
    fetch_far = pltpu.make_async_copy(one_table(tables_in, 1 - core), far_table, sems.at[1])
    near_at = out_ref.at[pl.ds(core * HALF, HALF), 0]
    far_at = out_ref.at[pl.ds((1 - core) * HALF, HALF), 0]
    near_out = pltpu.make_async_copy(near, near_at, sems.at[2])
    far_out = pltpu.make_async_copy(far_in, far_at, sems.at[3])
    late_out = pltpu.make_async_copy(far, far_at, sems.at[3])

    @pl.when(me != 1)
    def _():
        far_out.start()

    @pl.when(me == 1)
    def _():
        fetch_far.start()

    fill(store, 3 * core, halo_ref)
    fetch.wait()
    rows = columns_of(table_ref.__getitem__, 1 + core)

    def put(i, block):
        near[i] = block
        pltpu.make_async_copy(near.at[i], near_at.at[i], sems.at[2]).start()

    @pl.when(me == 0)
    def _():
        low_halo_squares(table_ref.__getitem__, store, rows, rounded(squares_ref, early_ref))
        cubes(table_ref.__getitem__, store, squares_ref, rows, put)

    @pl.when(me != 0)
    def _():
        squares(table_ref.__getitem__, store, 1 + core, rows, rounded(squares_ref))
        cubes(table_ref.__getitem__, store, squares_ref, rows, put)

    @pl.when(me == 1)
    def _():
        def put_far(i, block):
            far[i] = block

        fetch_far.wait()
        far_rows = columns_of(far_table.__getitem__, 2 - core)
        squares(far_table.__getitem__, store, 2 - core, far_rows, rounded(squares_ref))
        cubes(far_table.__getitem__, store, squares_ref, far_rows, put_far)
        late_out.start()
        late_out.wait()

    @pl.when(me != 1)
    def _():
        far_out.wait()

    near_out.wait()


def vmem():
    return pl.BlockSpec(memory_space=pltpu.VMEM)


def hbm():
    return pl.BlockSpec(memory_space=pltpu.HBM)


def call(kernel, name, args, in_specs, out_shape, out_specs, scratch_shapes=(), aliases=None):
    return pl.pallas_call(
        kernel,
        out_shape=out_shape,
        in_specs=in_specs,
        out_specs=out_specs,
        scratch_shapes=scratch_shapes,
        input_output_aliases=aliases or {},
        compiler_params=pltpu.CompilerParams(vmem_limit_bytes=16 * 1024 * 1024),
        cost_estimate=pl.CostEstimate(flops=0, bytes_accessed=0, transcendentals=0),
        name=name,
    )(*args)


def local(block_values, pattern_cols, pattern_counts):
    count = lax.axis_size("rows")
    to_core = [(i, i ^ 1) for i in range(count)]
    to_chip = [(i, (i + 1 if i % 2 else i - 1) % count) for i in range(count)]
    bf16, i32 = jnp.bfloat16, jnp.int32
    block_values = pltpu.with_memory_space_constraint(block_values, pltpu.HBM)
    rows = [pltpu.VMEM((HALF, 8, 64, 64), bf16)]
    sems = [pltpu.SemaphoreType.DMA((HALF // PIECE,))]
    packed = [jax.ShapeDtypeStruct((HALF * 4 * TILE + pad, 128), bf16) for pad in (PAD, 0)]
    cols, counts = pattern_cols.T, pattern_counts.reshape(-1, 128)
    cols, counts = (pltpu.with_memory_space_constraint(x, pltpu.HBM) for x in (cols, counts))
    pattern = [pltpu.VMEM(cols.shape, i32), pltpu.VMEM(counts.shape, i32), pltpu.SemaphoreType.DMA((2,))]
    stored = [jax.ShapeDtypeStruct(TABLES, i32), jax.ShapeDtypeStruct(STORE, bf16)]
    near, far, tables, store, early = call(
        pack_kernel,
        "pack",
        [block_values, cols, counts],
        [hbm()] * 3,
        packed + stored + [jax.ShapeDtypeStruct((HALF, 64, 512), jnp.float32)],
        [vmem()] * 5,
        rows * 2 + sems * 2 + pattern + [pltpu.SMEM(TABLES[1:], i32), pltpu.SemaphoreType.DMA],
    )
    far = call(
        rest_kernel,
        "rest",
        [block_values, far],
        [hbm(), vmem()],
        packed[1],
        vmem(),
        rows + sems,
        {1: 0},
    )
    near_halo = lax.ppermute(near, "rows", to_chip)
    far_halo = lax.ppermute(far, "rows", to_core)
    tables, store = call(
        own_kernel,
        "own",
        [near, far, cols, counts, tables, store],
        [vmem(), vmem(), hbm(), hbm(), vmem(), vmem()],
        stored,
        [vmem()] * 2,
        pattern,
        {4: 0, 5: 1},
    )
    tables = tables.reshape(-1)
    scratch = [
        pltpu.SMEM((TABLES[1] * TABLES[2],), i32),
        pltpu.VMEM((HALF, 64, 512), bf16),
        pltpu.SemaphoreType.DMA((4,)),
    ]
    far_result, store = call(
        far_kernel,
        "far_half",
        [tables, far_halo, store],
        [vmem()] * 3,
        [jax.ShapeDtypeStruct((HALF, 64, 64), bf16), stored[1]],
        [vmem()] * 2,
        scratch,
        {2: 1},
    )
    result, _ = call(
        near_kernel,
        "near_half",
        [tables, near_halo, far_result, early, store],
        [vmem()] * 5,
        [jax.ShapeDtypeStruct((2 * HALF, 1, 64, 64), bf16), stored[1]],
        [hbm(), vmem()],
        [scratch[0], *scratch, *[pltpu.VMEM((HALF, 64, 64), bf16)] * 2],
        {4: 1},
    )
    return result


def solution(mesh):
    in_specs = (P("rows", None, None, None), P(), P())
    out_specs = P("rows", "rep", None, None)
    return jax.shard_map(local, mesh=mesh, in_specs=in_specs, out_specs=out_specs, check_vma=False)
```

time: 27.4 us -> 27.4 us (level)
  starting transfers between devices: 19.2 us -> 19.5 us
  transfers between devices with their start and end apart: 2 -> 2, of which waited for: 1 -> 1; matrix products, arithmetic and copies ran while one was open for 0% -> 0% of each run, Pallas kernels for 8% -> 7%
where the time goes in v6:
time: 27.4 us; the launch traced here: 27.2 us
  starting transfers between devices  19.5 us (71%)
  Pallas kernels  7.61 us (28%)
    ppermute x1, starting transfers between devices, local(): far_halo = lax.ppermute(far, 'rows', to_core)  14.9 us
    pallas_call x5, Pallas kernels, call(): pl.pallas_call(kernel, out_shape=out_shape, in_specs=in_specs, out_specs=...  7.61 us
    ppermute x1, starting transfers between devices, local(): near_halo = lax.ppermute(near, 'rows', to_chip)  4.51 us
  transfers between devices with their start and end apart: 2, of which 1 were waited for; matrix products, arithmetic and copies ran while one was open for 0% of the time, Pallas kernels for 7%

profile of v6, /device:TPU:1, one launch (start us, length us, event | category | flops | bytes accessed | tf_op | source)
XLA Modules:
  0.0 27.2 jit_solution(1126536180119785600)
XLA Ops:
  0.0 1.8 %pack.1 = (bf16[2064,128]{1,0:T(8,128)(2,1)S(1)}, bf16[2048,128]{1,0:T(8,128)(2,1)S(1)}, s32[2,8,128]{2,1,0:T(8,128)S(1)}, bf16[392,64,128]{2,1,0:T(8,128)(2,1)S(1)}, f32[8,64,512]{2,1,0:T(8,128)S(1)}) custom-call(bf16[16,8,64,64]{3,2,1,0:T(8,128)(2,1)} %x_ref.3, s32[8,1536]{1,0:T(8,128)} %bitcast.5, s32[12,128]{1,0:T(8,128)} %bitcast.7), custom_call_target="tpu_custom_call" | custom-call | tf_op jit(solution)/shard_map/pack/pallas_call | solution.py:358
  1.8 4.5 %collective-permute-start = (bf16[2064,128]{1,0:T(8,128)(2,1)S(1)}, bf16[2064,128]{1,0:T(8,128)(2,1)S(1)}, u32[]{:S(2)}, u32[]{:S(2)}) collective-permute-start(bf16[2064,128]{1,0:T(8,128)(2,1)S(1)} %get-tuple-element.15.near_ref), channel_id=1, source_target_pairs={{0,760},{8,16},{16,8},{24,32},{32,24},{40,48},{48,40},{56,64},{64,... | collective-permute-start | bytes 1585160 | tf_op jit(solution)/shard_map/ppermute | solution.py:403
  6.4 14.9 %collective-permute-start.1 = (bf16[2048,128]{1,0:T(8,128)(2,1)S(1)}, bf16[2048,128]{1,0:T(8,128)(2,1)S(1)}, u32[]{:S(2)}, u32[]{:S(2)}) collective-permute-start(bf16[2048,128]{1,0:T(8,128)(2,1)S(1)} %rest.1.far_ref), channel_id=1, source_target_pairs={{0,8},{8,0},{16,24},{24,16},{32,40},{40,32},{48,56},{56,48},{64,72... | collective-permute-start | bytes 1572872 | tf_op jit(solution)/shard_map/ppermute | solution.py:404
  21.4 1.4 %own.1 = (s32[2,8,128]{2,1,0:T(8,128)S(1)}, bf16[392,64,128]{2,1,0:T(8,128)(2,1)S(1)}) custom-call(bf16[2064,128]{1,0:T(8,128)(2,1)S(1)} %get-tuple-element.15.near_ref, bf16[2048,128]{1,0:T(8,128)(2,1)S(1)} %rest.1.far_ref, s32[8,1536]{1,0:T(8,128)} %bitcast.6, s32[12,128]{1,0:T(8,128)} %bitcast.8, ...), custom_call_target="tpu_custom_call", output_to_operand_aliasing={{0}: (4, {}), {1}: (5, {})} | custom-call | tf_op jit(solution)/shard_map/own/pallas_call | solution.py:358
  22.8 0.1 collective-permute-done.1.halo_ref
  22.9 0.4 %far_half.1 = (bf16[8,64,64]{2,1,0:T(8,128)(2,1)S(1)}, bf16[392,64,128]{2,1,0:T(8,128)(2,1)S(1)}) custom-call(s32[2048]{0:T(1024)S(1)} %bitcast.3, bf16[2048,128]{1,0:T(8,128)(2,1)S(1)} %collective-permute-done.1.halo_ref, bf16[392,64,128]{2,1,0:T(8,128)(2,1)S(1)} %get-tuple-element.20._), custom_call_target="tpu_custom_call", output_to_operand_aliasing={{1}: (2, {})} | custom-call | tf_op jit(solution)/shard_map/far_half/pallas_call | solution.py:358
  23.2 0.0 collective-permute-done.halo_ref
  23.2 4.0 %near_half.1 = (bf16[16,1,64,64]{3,2,1,0:T(8,128)(2,1)}, bf16[392,64,128]{2,1,0:T(8,128)(2,1)S(1)}) custom-call(s32[2048]{0:T(1024)S(1)} %bitcast.4, bf16[2064,128]{1,0:T(8,128)(2,1)S(1)} %collective-permute-done.halo_ref, bf16[8,64,64]{2,1,0:T(8,128)(2,1)S(1)} %get-tuple-element.21.far_in, ...), custom_call_target="tpu_custom_call", output_to_operand_aliasing={{1}: (4, {})} | custom-call | tf_op jit(solution)/shard_map/near_half/pallas_call | solution.py:358
  (1 shorter events, 0.0 us)
Async XLA Ops:
  1.8 21.4 %collective-permute-start = (bf16[2064,128]{1,0:T(8,128)(2,1)S(1)}, bf16[2064,128]{1,0:T(8,128)(2,1)S(1)}, u32[]{:S(2)}, u32[]{:S(2)}) collective-permute-start(bf16[2064,128]{1,0:T(8,128)(2,1)S(1)} %get-tuple-element.15.near_ref), channel_id=1, source_target_pairs={{0,760},{8,16},{16,8},{24,32},{32,24},{40,48},{48,40},{56,64},{64,... | collective-permute-start | bytes 1585160 | tf_op jit(solution)/shard_map/ppermute | solution.py:403
  6.4 16.5 %collective-permute-start.1 = (bf16[2048,128]{1,0:T(8,128)(2,1)S(1)}, bf16[2048,128]{1,0:T(8,128)(2,1)S(1)}, u32[]{:S(2)}, u32[]{:S(2)}) collective-permute-start(bf16[2048,128]{1,0:T(8,128)(2,1)S(1)} %rest.1.far_ref), channel_id=1, source_target_pairs={{0,8},{8,0},{16,24},{24,16},{32,40},{40,32},{48,56},{56,48},{64,72... | collective-permute-start | bytes 1572872 | tf_op jit(solution)/shard_map/ppermute | solution.py:404

commit v7 on v6

--- a/solution.py
+++ b/solution.py
@@ -197,6 +197,10 @@
         squares_ref[i, :, at] = total.astype(jnp.bfloat16)
 
     return put
+
+
+def waits_longest():
+    return (lax.axis_index("rows") == 0) & (lax.axis_index("rep") != 0)
 
 
 def pack_kernel(
@@ -238,7 +242,7 @@
     def _():
         pack(far, far_rows, far_ref)
 
-    @pl.when(me == 0)
+    @pl.when(waits_longest())
     def _():
         own(near_ref, far_ref, cols_in, counts_in, tables_ref, store, cols_ref, counts_ref, own_sems)
         fetch = pltpu.make_async_copy(tables_ref.at[0], table_ref, fetch_sem)
@@ -255,7 +259,7 @@
 
 
 def own_kernel(near_ref, far_ref, cols_in, counts_in, _, __, tables_ref, store, cols_ref, counts_ref, sems):
-    @pl.when(lax.axis_index("rows") != 0)
+    @pl.when(jnp.logical_not(waits_longest()))
     def _():
         own(near_ref, far_ref, cols_in, counts_in, tables_ref, store, cols_ref, counts_ref, sems)
 
@@ -317,12 +321,12 @@
         near[i] = block
         pltpu.make_async_copy(near.at[i], near_at.at[i], sems.at[2]).start()
 
-    @pl.when(me == 0)
+    @pl.when(waits_longest())
     def _():
         low_halo_squares(table_ref.__getitem__, store, rows, rounded(squares_ref, early_ref))
         cubes(table_ref.__getitem__, store, squares_ref, rows, put)
 
-    @pl.when(me != 0)
+    @pl.when(jnp.logical_not(waits_longest()))
     def _():
         squares(table_ref.__getitem__, store, 1 + core, rows, rounded(squares_ref))
         cubes(table_ref.__getitem__, store, squares_ref, rows, put)

time: 27.4 us -> 27.2 us (level)
  starting transfers between devices: 19.5 us -> 19.2 us
where the time goes in v7:
time: 27.2 us; the launch traced here: 26.9 us
  starting transfers between devices  19.2 us (71%)
  Pallas kernels  7.61 us (28%)
    ppermute x1, starting transfers between devices, local(): far_halo = lax.ppermute(far, 'rows', to_core)  14.7 us
    pallas_call x5, Pallas kernels, call(): pl.pallas_call(kernel, out_shape=out_shape, in_specs=in_specs, out_specs=...  7.61 us
    ppermute x1, starting transfers between devices, local(): near_halo = lax.ppermute(near, 'rows', to_chip)  4.51 us
  transfers between devices with their start and end apart: 2, of which 1 were waited for; matrix products, arithmetic and copies ran while one was open for 0% of the time, Pallas kernels for 7%

profile of v7, /device:TPU:1, one launch (start us, length us, event | category | flops | bytes accessed | tf_op | source)
XLA Modules:
  0.0 26.9 jit_solution(9696108729696397455)
XLA Ops:
  0.0 1.8 %pack.1 = (bf16[2064,128]{1,0:T(8,128)(2,1)S(1)}, bf16[2048,128]{1,0:T(8,128)(2,1)S(1)}, s32[2,8,128]{2,1,0:T(8,128)S(1)}, bf16[392,64,128]{2,1,0:T(8,128)(2,1)S(1)}, f32[8,64,512]{2,1,0:T(8,128)S(1)}) custom-call(bf16[16,8,64,64]{3,2,1,0:T(8,128)(2,1)} %x_ref.3, s32[8,1536]{1,0:T(8,128)} %bitcast.5, s32[12,128]{1,0:T(8,128)} %bitcast.7), custom_call_target="tpu_custom_call" | custom-call | tf_op jit(solution)/shard_map/pack/pallas_call | solution.py:362
  1.8 4.5 %collective-permute-start = (bf16[2064,128]{1,0:T(8,128)(2,1)S(1)}, bf16[2064,128]{1,0:T(8,128)(2,1)S(1)}, u32[]{:S(2)}, u32[]{:S(2)}) collective-permute-start(bf16[2064,128]{1,0:T(8,128)(2,1)S(1)} %get-tuple-element.15.near_ref), channel_id=1, source_target_pairs={{0,760},{8,16},{16,8},{24,32},{32,24},{40,48},{48,40},{56,64},{64,... | collective-permute-start | bytes 1585160 | tf_op jit(solution)/shard_map/ppermute | solution.py:407
  6.4 14.7 %collective-permute-start.1 = (bf16[2048,128]{1,0:T(8,128)(2,1)S(1)}, bf16[2048,128]{1,0:T(8,128)(2,1)S(1)}, u32[]{:S(2)}, u32[]{:S(2)}) collective-permute-start(bf16[2048,128]{1,0:T(8,128)(2,1)S(1)} %rest.1.far_ref), channel_id=1, source_target_pairs={{0,8},{8,0},{16,24},{24,16},{32,40},{40,32},{48,56},{56,48},{64,72... | collective-permute-start | bytes 1572872 | tf_op jit(solution)/shard_map/ppermute | solution.py:408
  21.1 1.4 %own.1 = (s32[2,8,128]{2,1,0:T(8,128)S(1)}, bf16[392,64,128]{2,1,0:T(8,128)(2,1)S(1)}) custom-call(bf16[2064,128]{1,0:T(8,128)(2,1)S(1)} %get-tuple-element.15.near_ref, bf16[2048,128]{1,0:T(8,128)(2,1)S(1)} %rest.1.far_ref, s32[8,1536]{1,0:T(8,128)} %bitcast.6, s32[12,128]{1,0:T(8,128)} %bitcast.8, ...), custom_call_target="tpu_custom_call", output_to_operand_aliasing={{0}: (4, {}), {1}: (5, {})} | custom-call | tf_op jit(solution)/shard_map/own/pallas_call | solution.py:362
  22.5 0.1 collective-permute-done.1.halo_ref
  22.6 0.4 %far_half.1 = (bf16[8,64,64]{2,1,0:T(8,128)(2,1)S(1)}, bf16[392,64,128]{2,1,0:T(8,128)(2,1)S(1)}) custom-call(s32[2048]{0:T(1024)S(1)} %bitcast.3, bf16[2048,128]{1,0:T(8,128)(2,1)S(1)} %collective-permute-done.1.halo_ref, bf16[392,64,128]{2,1,0:T(8,128)(2,1)S(1)} %get-tuple-element.20._), custom_call_target="tpu_custom_call", output_to_operand_aliasing={{1}: (2, {})} | custom-call | tf_op jit(solution)/shard_map/far_half/pallas_call | solution.py:362
  23.0 0.0 collective-permute-done.halo_ref
  23.0 4.0 %near_half.1 = (bf16[16,1,64,64]{3,2,1,0:T(8,128)(2,1)}, bf16[392,64,128]{2,1,0:T(8,128)(2,1)S(1)}) custom-call(s32[2048]{0:T(1024)S(1)} %bitcast.4, bf16[2064,128]{1,0:T(8,128)(2,1)S(1)} %collective-permute-done.halo_ref, bf16[8,64,64]{2,1,0:T(8,128)(2,1)S(1)} %get-tuple-element.21.far_in, ...), custom_call_target="tpu_custom_call", output_to_operand_aliasing={{1}: (4, {})} | custom-call | tf_op jit(solution)/shard_map/near_half/pallas_call | solution.py:362
  (1 shorter events, 0.0 us)
Async XLA Ops:
  1.8 21.1 %collective-permute-start = (bf16[2064,128]{1,0:T(8,128)(2,1)S(1)}, bf16[2064,128]{1,0:T(8,128)(2,1)S(1)}, u32[]{:S(2)}, u32[]{:S(2)}) collective-permute-start(bf16[2064,128]{1,0:T(8,128)(2,1)S(1)} %get-tuple-element.15.near_ref), channel_id=1, source_target_pairs={{0,760},{8,16},{16,8},{24,32},{32,24},{40,48},{48,40},{56,64},{64,... | collective-permute-start | bytes 1585160 | tf_op jit(solution)/shard_map/ppermute | solution.py:407
  6.4 16.2 %collective-permute-start.1 = (bf16[2048,128]{1,0:T(8,128)(2,1)S(1)}, bf16[2048,128]{1,0:T(8,128)(2,1)S(1)}, u32[]{:S(2)}, u32[]{:S(2)}) collective-permute-start(bf16[2048,128]{1,0:T(8,128)(2,1)S(1)} %rest.1.far_ref), channel_id=1, source_target_pairs={{0,8},{8,0},{16,24},{24,16},{32,40},{40,32},{48,56},{56,48},{64,72... | collective-permute-start | bytes 1572872 | tf_op jit(solution)/shard_map/ppermute | solution.py:408

commit v8 on v7

v8 whole, which is shorter than its diff:
```python
import jax
import jax.numpy as jnp
from jax import lax
from jax.experimental import pallas as pl
from jax.experimental.pallas import tpu as pltpu
from jax.sharding import PartitionSpec as P

HALF = 8
PIECE = 4
WINDOW = 32
TILE = 64
PAD = 16
GROUP = 12
ZERO_TILE = WINDOW * GROUP
STORE = (ZERO_TILE + 8, TILE, 128)
ALL, EARLY, LOW, LOW_X = range(4)
LISTS = (4, 8, 128)


def fill(store, chunk, ref):
    for row in range(HALF):
        base = (chunk * HALF + row) * GROUP
        for pair in range(4):
            tile = ref[pl.ds((row * 4 + pair) * TILE, TILE), :]
            store[base + pair] = tile
            store[base + 4 + pair] = pltpu.roll(tile, 64, 1)
            store[base + 8 + pair] = tile


def from_pieces(x_ref, rows, sems, starts):
    return [
        pltpu.make_async_copy(x_ref.at[pl.ds(start, PIECE)], rows.at[pl.ds(n * PIECE, PIECE)], sems.at[n])
        for n, start in enumerate(starts)
    ]


def pack(copies, rows, out_ref):
    for n, copy in enumerate(copies):
        copy.wait()
        for row in range(n * PIECE, (n + 1) * PIECE):
            for pair in range(4):
                at = pl.ds((row * 4 + pair) * TILE, TILE)
                blocks = [rows[row, 2 * pair + side] for side in range(2)]
                out_ref[at, :] = jnp.concatenate(blocks, axis=1)


def rest_kernel(x_ref, _, far_ref, far_rows, far_sems):
    me = lax.axis_index("rows")
    core = lax.rem(me, 2)

    @pl.when(me == lax.axis_size("rows") - 1)
    def _():
        far = from_pieces(x_ref, far_rows, far_sems, ((1 - core) * HALF, (1 - core) * HALF + PIECE))
        for copy in far:
            copy.start()
        pack(far, far_rows, far_ref)


def own(near_ref, far_ref, cols_in, counts_in, lists_ref, store, cols_ref, counts_ref, sems):
    copies = [
        pltpu.make_async_copy(cols_in, cols_ref, sems.at[0]),
        pltpu.make_async_copy(counts_in, counts_ref, sems.at[1]),
    ]
    for copy in copies:
        copy.start()
    core = lax.rem(lax.axis_index("rows"), 2)
    zeros = jnp.zeros((TILE, 128), jnp.bfloat16)
    store[ZERO_TILE] = zeros
    store[ZERO_TILE + 4] = zeros
    fill(store, 1 + core, near_ref)
    fill(store, 2 - core, far_ref)
    for copy in copies:
        copy.wait()
    total = cols_ref.shape[1]
    chunks = total // 128
    start = lax.rem(lax.axis_index("rows") * (2 * HALF) + (total - HALF), total)
    first = lax.div(start, 128)
    second = lax.rem(first + 1, chunks)
    shift = lax.rem(256 - lax.rem(start, 128), 256)

    def window(get):
        both = jnp.concatenate([get(first), get(second)], axis=1)
        return pltpu.roll(both, shift, 1)[:, :128]

    cols = window(lambda k: cols_ref[:, pl.ds(pl.multiple_of(k * 128, 128), 128)])
    counts = window(lambda k: jnp.broadcast_to(counts_ref[pl.ds(k, 1), :], (8, 128)))
    relative = cols - start
    relative = jnp.where(relative < 0, relative + total, relative)
    slot = lax.broadcasted_iota(jnp.int32, (8, 128), 0)
    lane = lax.broadcasted_iota(jnp.int32, (8, 128), 1)
    live = (slot < counts) & (lane < WINDOW) & (relative < WINDOW)
    columns = jnp.where(live, relative, -1)
    side = (slot % 2) * 4 + slot // 2
    mine = lax.axis_index("rep")

    def at_lanes(which):
        return jnp.take_along_axis(columns, which, axis=1, mode="promise_in_bounds")

    def highest(x):
        return jnp.broadcast_to(jnp.max(x, axis=0, keepdims=True), (8, 128))

    def tiles(own, row):
        found = at_lanes(jnp.maximum(row, 0))
        result = jnp.full((8, 128), ZERO_TILE, jnp.int32)
        for q in range(8):
            wanted = highest(jnp.where(slot == (mine ^ q), own, -1))
            match = (found == wanted) & (wanted >= 0) & (row >= 0)
            tile = highest(jnp.where(match, row * GROUP + side, -1))
            result = jnp.where((slot == q) & (tile >= 0), tile, result)
        return result

    own_row = HALF + lane // 8
    own_columns = at_lanes(own_row)
    source = highest(jnp.where(slot == ((lane % 8) ^ mine), own_columns, -1))
    everything = tiles(own_columns, source)
    lists_ref[ALL] = everything
    lists_ref[EARLY] = jnp.where(source < HALF, ZERO_TILE, everything)
    lists_ref[LOW] = tiles(own_columns, lane % 8)
    low_x = highest(jnp.where(own_columns == lane % 8, own_row * GROUP + side, -1))
    lists_ref[LOW_X] = jnp.where(low_x >= 0, low_x, ZERO_TILE)


def half_list(lists_ref, center):
    return jnp.where(center == 1, lists_ref[ALL], pltpu.roll(lists_ref[ALL], 64, 1))


def product(x, tiles, store, sources, n):
    left = lax.broadcasted_iota(jnp.int16, (TILE, 128), 1) < 64

    def tile(p, b):
        if b is None:
            return jnp.zeros((TILE, 128), jnp.bfloat16)
        return jnp.where(left, store[tiles[2 * p, b]], store[tiles[2 * p + 1, b] + 4])

    total = None
    for k in range(0, len(sources), 4):
        g = jnp.concatenate(
            [
                jnp.concatenate([tile(2 * n + j, b) for j in range(2)], axis=1)
                for b in sources[k : k + 4]
            ],
            axis=0,
        )
        part = jnp.dot(x[:, k * 64 : (k + 4) * 64], g, preferred_element_type=jnp.float32)
        total = part if total is None else total + part
    return total


def squares(tiles, store, center, put):
    mine = lax.axis_index("rep")
    for i in range(HALF):
        at = (center * HALF + i) * GROUP + lax.rem(mine, 2) * 4
        x = jnp.concatenate([store[at + (lax.div(mine, 2) ^ p)] for p in range(4)], axis=1)
        for n in range(2):
            put(i, n, product(x, tiles, store, [i * 8 + b for b in range(8)], n))


def low_halo_squares(lists_ref, store, put):
    tiles, own_tiles = lists_ref[LOW], lists_ref[LOW_X]
    left = lax.broadcasted_iota(jnp.int16, (TILE, 128), 1) < 64
    for i in range(HALF):
        sources = [i * 8 + w for w in range(i, HALF)] + [None] * (i % 2)
        found = [ZERO_TILE if b is None else own_tiles[0, b] for b in sources]
        x = jnp.concatenate(
            [
                jnp.where(left, store[found[k]], store[found[k + 1] + 4])
                for k in range(0, len(sources), 2)
            ],
            axis=1,
        )
        for n in range(2):
            put(i, n, product(x, tiles, store, sources, n))


def cubes(tiles, store, squares_ref, put):
    for i in range(HALF):
        cube = None
        for k in range(2):
            g = jnp.concatenate([store[tiles[0, i * 8 + 4 * k + b]] for b in range(4)], axis=0)
            part = jnp.dot(
                squares_ref[i, :, k * 256 : (k + 1) * 256], g, preferred_element_type=jnp.float32
            )
            cube = part if cube is None else cube + part
        purified = 3.0 * squares_ref[i, :, 0:128].astype(jnp.float32) - 2.0 * cube
        put(i, purified[:, :64].astype(jnp.bfloat16))


def rounded(squares_ref, before=None):
    def put(i, n, total):
        at = slice(n * 256, (n + 1) * 256)
        if before is not None:
            total = total + before[i, :, at]
        squares_ref[i, :, at] = total.astype(jnp.bfloat16)

    return put


def waits_longest():
    return (lax.axis_index("rows") == 0) & (lax.axis_index("rep") != 0)


def pack_kernel(
    x_ref,
    cols_in,
    counts_in,
    near_ref,
    far_ref,
    lists_ref,
    store,
    early_ref,
    near_rows,
    far_rows,
    near_sems,
    far_sems,
    cols_ref,
    counts_ref,
    own_sems,
):
    me = lax.axis_index("rows")
    core = lax.rem(me, 2)
    late = me == lax.axis_size("rows") - 1
    near = from_pieces(x_ref, near_rows, near_sems, (core * HALF, core * HALF + PIECE))
    far = from_pieces(x_ref, far_rows, far_sems, ((1 - core) * HALF, (1 - core) * HALF + PIECE))
    for copy in near:
        copy.start()

    @pl.when(jnp.logical_not(late))
    def _():
        for copy in far:
            copy.start()

    near_ref[HALF * 4 * TILE :, :] = jnp.zeros((PAD, 128), jnp.bfloat16)
    pack(near, near_rows, near_ref)

    @pl.when(jnp.logical_not(late))
    def _():
        pack(far, far_rows, far_ref)

    @pl.when(waits_longest())
    def _():
        own(near_ref, far_ref, cols_in, counts_in, lists_ref, store, cols_ref, counts_ref, own_sems)

        def put(i, n, total):
            early_ref[i, :, n * 256 : (n + 1) * 256] = total

        squares(lists_ref[EARLY], store, 1, put)


def own_kernel(near_ref, far_ref, cols_in, counts_in, _, __, lists_ref, store, cols_ref, counts_ref, sems):
    @pl.when(jnp.logical_not(waits_longest()))
    def _():
        own(near_ref, far_ref, cols_in, counts_in, lists_ref, store, cols_ref, counts_ref, sems)


def far_kernel(lists_ref, halo_ref, _, out_ref, store, squares_ref):
    me = lax.axis_index("rows")
    core = lax.rem(me, 2)
    fill(store, 3 * (1 - core), halo_ref)

    def put(i, block):
        out_ref[i] = block

    @pl.when(me != 1)
    def _():
        tiles = half_list(lists_ref, 2 - core)
        squares(tiles, store, 2 - core, rounded(squares_ref))
        cubes(tiles, store, squares_ref, put)


def near_kernel(lists_ref, halo_ref, far_in, early_ref, _, out_ref, store, squares_ref, near, far, sems):
    me = lax.axis_index("rows")
    core = lax.rem(me, 2)
    near_at = out_ref.at[pl.ds(core * HALF, HALF), 0]
    far_at = out_ref.at[pl.ds((1 - core) * HALF, HALF), 0]
    near_out = pltpu.make_async_copy(near, near_at, sems.at[0])
    far_out = pltpu.make_async_copy(far_in, far_at, sems.at[1])
    late_out = pltpu.make_async_copy(far, far_at, sems.at[1])

    @pl.when(me != 1)
    def _():
        far_out.start()

    fill(store, 3 * core, halo_ref)

    def put(i, block):
        near[i] = block

    @pl.when(waits_longest())
    def _():
        low_halo_squares(lists_ref, store, rounded(squares_ref, early_ref))
        cubes(lists_ref[ALL], store, squares_ref, put)

    @pl.when(jnp.logical_not(waits_longest()))
    def _():
        tiles = half_list(lists_ref, 1 + core)
        squares(tiles, store, 1 + core, rounded(squares_ref))
        cubes(tiles, store, squares_ref, put)

    near_out.start()

    @pl.when(me == 1)
    def _():
        def put_far(i, block):
            far[i] = block

        tiles = half_list(lists_ref, 2 - core)
        squares(tiles, store, 2 - core, rounded(squares_ref))
        cubes(tiles, store, squares_ref, put_far)
        late_out.start()
        late_out.wait()

    @pl.when(me != 1)
    def _():
        far_out.wait()

    near_out.wait()


def vmem():
    return pl.BlockSpec(memory_space=pltpu.VMEM)


def hbm():
    return pl.BlockSpec(memory_space=pltpu.HBM)


def call(kernel, name, args, in_specs, out_shape, out_specs, scratch_shapes=(), aliases=None):
    return pl.pallas_call(
        kernel,
        out_shape=out_shape,
        in_specs=in_specs,
        out_specs=out_specs,
        scratch_shapes=scratch_shapes,
        input_output_aliases=aliases or {},
        compiler_params=pltpu.CompilerParams(vmem_limit_bytes=16 * 1024 * 1024),
        cost_estimate=pl.CostEstimate(flops=0, bytes_accessed=0, transcendentals=0),
        name=name,
    )(*args)


def local(block_values, pattern_cols, pattern_counts):
    count = lax.axis_size("rows")
    to_core = [(i, i ^ 1) for i in range(count)]
    to_chip = [(i, (i + 1 if i % 2 else i - 1) % count) for i in range(count)]
    bf16, i32 = jnp.bfloat16, jnp.int32
    block_values = pltpu.with_memory_space_constraint(block_values, pltpu.HBM)
    rows = [pltpu.VMEM((HALF, 8, 64, 64), bf16)]
    sems = [pltpu.SemaphoreType.DMA((HALF // PIECE,))]
    packed = [jax.ShapeDtypeStruct((HALF * 4 * TILE + pad, 128), bf16) for pad in (PAD, 0)]
    cols, counts = pattern_cols.T, pattern_counts.reshape(-1, 128)
    cols, counts = (pltpu.with_memory_space_constraint(x, pltpu.HBM) for x in (cols, counts))
    pattern = [pltpu.VMEM(cols.shape, i32), pltpu.VMEM(counts.shape, i32), pltpu.SemaphoreType.DMA((2,))]
    stored = [jax.ShapeDtypeStruct(LISTS, i32), jax.ShapeDtypeStruct(STORE, bf16)]
    near, far, lists, store, early = call(
        pack_kernel,
        "pack",
        [block_values, cols, counts],
        [hbm()] * 3,
        packed + stored + [jax.ShapeDtypeStruct((HALF, 64, 512), jnp.float32)],
        [vmem()] * 5,
        rows * 2 + sems * 2 + pattern,
    )
    far = call(
        rest_kernel,
        "rest",
        [block_values, far],
        [hbm(), vmem()],
        packed[1],
        vmem(),
        rows + sems,
        {1: 0},
    )
    near_halo = lax.ppermute(near, "rows", to_chip)
    far_halo = lax.ppermute(far, "rows", to_core)
    lists, store = call(
        own_kernel,
        "own",
        [near, far, cols, counts, lists, store],
        [vmem(), vmem(), hbm(), hbm(), vmem(), vmem()],
        stored,
        [vmem()] * 2,
        pattern,
        {4: 0, 5: 1},
    )
    scratch = [pltpu.VMEM((HALF, 64, 512), bf16)]
    far_result, store = call(
        far_kernel,
        "far_half",
        [lists, far_halo, store],
        [vmem()] * 3,
        [jax.ShapeDtypeStruct((HALF, 64, 64), bf16), stored[1]],
        [vmem()] * 2,
        scratch,
        {2: 1},
    )
    result, _ = call(
        near_kernel,
        "near_half",
        [lists, near_halo, far_result, early, store],
        [vmem()] * 5,
        [jax.ShapeDtypeStruct((2 * HALF, 1, 64, 64), bf16), stored[1]],
        [hbm(), vmem()],
        scratch + [pltpu.VMEM((HALF, 64, 64), bf16)] * 2 + [pltpu.SemaphoreType.DMA((2,))],
        {4: 1},
    )
    return result


def solution(mesh):
    in_specs = (P("rows", None, None, None), P(), P())
    out_specs = P("rows", "rep", None, None)
    return jax.shard_map(local, mesh=mesh, in_specs=in_specs, out_specs=out_specs, check_vma=False)
```

time: 27.2 us -> 26.9 us (0.989)
  transfers between devices with their start and end apart: 2 -> 2, of which waited for: 1 -> 0; matrix products, arithmetic and copies ran while one was open for 0% -> 0% of each run, Pallas kernels for 7% -> 7%
where the time goes in v8:
time: 26.9 us; the launch traced here: 26.7 us
  starting transfers between devices  19.2 us (71%)
  Pallas kernels  7.41 us (28%)
    ppermute x1, starting transfers between devices, local(): far_halo = lax.ppermute(far, 'rows', to_core)  14.7 us
    pallas_call x5, Pallas kernels, call(): pl.pallas_call(kernel, out_shape=out_shape, in_specs=in_specs, out_specs=...  7.41 us
    ppermute x1, starting transfers between devices, local(): near_halo = lax.ppermute(near, 'rows', to_chip)  4.51 us
  transfers between devices with their start and end apart: 2, of which 0 were waited for; matrix products, arithmetic and copies ran while one was open for 0% of the time, Pallas kernels for 7%

profile of v8, /device:TPU:1, one launch (start us, length us, event | category | flops | bytes accessed | tf_op | source)
XLA Modules:
  0.0 26.7 jit_solution(13968975830942709909)
XLA Ops:
  0.0 1.8 %pack.1 = (bf16[2064,128]{1,0:T(8,128)(2,1)S(1)}, bf16[2048,128]{1,0:T(8,128)(2,1)S(1)}, s32[4,8,128]{2,1,0:T(8,128)S(1)}, bf16[392,64,128]{2,1,0:T(8,128)(2,1)S(1)}, f32[8,64,512]{2,1,0:T(8,128)S(1)}) custom-call(bf16[16,8,64,64]{3,2,1,0:T(8,128)(2,1)} %x_ref.3, s32[8,1536]{1,0:T(8,128)} %bitcast.2, s32[12,128]{1,0:T(8,128)} %bitcast.4), custom_call_target="tpu_custom_call" | custom-call | tf_op jit(solution)/shard_map/pack/pallas_call | solution.py:328
  1.8 4.5 %collective-permute-start = (bf16[2064,128]{1,0:T(8,128)(2,1)S(1)}, bf16[2064,128]{1,0:T(8,128)(2,1)S(1)}, u32[]{:S(2)}, u32[]{:S(2)}) collective-permute-start(bf16[2064,128]{1,0:T(8,128)(2,1)S(1)} %get-tuple-element.15.near_ref), channel_id=1, source_target_pairs={{0,760},{8,16},{16,8},{24,32},{32,24},{40,48},{48,40},{56,64},{64,... | collective-permute-start | bytes 1585160 | tf_op jit(solution)/shard_map/ppermute | solution.py:373
  6.4 14.7 %collective-permute-start.1 = (bf16[2048,128]{1,0:T(8,128)(2,1)S(1)}, bf16[2048,128]{1,0:T(8,128)(2,1)S(1)}, u32[]{:S(2)}, u32[]{:S(2)}) collective-permute-start(bf16[2048,128]{1,0:T(8,128)(2,1)S(1)} %rest.1.far_ref), channel_id=1, source_target_pairs={{0,8},{8,0},{16,24},{24,16},{32,40},{40,32},{48,56},{56,48},{64,72... | collective-permute-start | bytes 1572872 | tf_op jit(solution)/shard_map/ppermute | solution.py:374
  21.1 1.5 %own.1 = (s32[4,8,128]{2,1,0:T(8,128)S(1)}, bf16[392,64,128]{2,1,0:T(8,128)(2,1)S(1)}) custom-call(bf16[2064,128]{1,0:T(8,128)(2,1)S(1)} %get-tuple-element.15.near_ref, bf16[2048,128]{1,0:T(8,128)(2,1)S(1)} %rest.1.far_ref, s32[8,1536]{1,0:T(8,128)} %bitcast.3, s32[12,128]{1,0:T(8,128)} %bitcast.5, ...), custom_call_target="tpu_custom_call", output_to_operand_aliasing={{0}: (4, {}), {1}: (5, {})} | custom-call | tf_op jit(solution)/shard_map/own/pallas_call | solution.py:328
  22.6 0.0 collective-permute-done.1.halo_ref
  22.6 0.3 %far_half.1 = (bf16[8,64,64]{2,1,0:T(8,128)(2,1)S(1)}, bf16[392,64,128]{2,1,0:T(8,128)(2,1)S(1)}) custom-call(s32[4,8,128]{2,1,0:T(8,128)S(1)} %get-tuple-element.19.lists_ref, bf16[2048,128]{1,0:T(8,128)(2,1)S(1)} %collective-permute-done.1.halo_ref, bf16[392,64,128]{2,1,0:T(8,128)(2,1)S(1)} %get-tuple-element.20._), custom_call_target="tpu_custom_call", output_to_operand_aliasing={{1}: (2, {})} | custom-call | tf_op jit(solution)/shard_map/far_half/pallas_call | solution.py:328
  23.0 0.0 collective-permute-done.halo_ref
  23.0 3.7 %near_half.1 = (bf16[16,1,64,64]{3,2,1,0:T(8,128)(2,1)}, bf16[392,64,128]{2,1,0:T(8,128)(2,1)S(1)}) custom-call(s32[4,8,128]{2,1,0:T(8,128)S(1)} %get-tuple-element.19.lists_ref, bf16[2064,128]{1,0:T(8,128)(2,1)S(1)} %collective-permute-done.halo_ref, bf16[8,64,64]{2,1,0:T(8,128)(2,1)S(1)} %get-tuple-element.21.far_in, ...), custom_call_target="tpu_custom_call", output_to_operand_aliasing={{1}: (4, {})} | custom-call | tf_op jit(solution)/shard_map/near_half/pallas_call | solution.py:328
  (1 shorter events, 0.0 us)
Async XLA Ops:
  1.8 21.1 %collective-permute-start = (bf16[2064,128]{1,0:T(8,128)(2,1)S(1)}, bf16[2064,128]{1,0:T(8,128)(2,1)S(1)}, u32[]{:S(2)}, u32[]{:S(2)}) collective-permute-start(bf16[2064,128]{1,0:T(8,128)(2,1)S(1)} %get-tuple-element.15.near_ref), channel_id=1, source_target_pairs={{0,760},{8,16},{16,8},{24,32},{32,24},{40,48},{48,40},{56,64},{64,... | collective-permute-start | bytes 1585160 | tf_op jit(solution)/shard_map/ppermute | solution.py:373
  6.4 16.2 %collective-permute-start.1 = (bf16[2048,128]{1,0:T(8,128)(2,1)S(1)}, bf16[2048,128]{1,0:T(8,128)(2,1)S(1)}, u32[]{:S(2)}, u32[]{:S(2)}) collective-permute-start(bf16[2048,128]{1,0:T(8,128)(2,1)S(1)} %rest.1.far_ref), channel_id=1, source_target_pairs={{0,8},{8,0},{16,24},{24,16},{32,40},{40,32},{48,56},{56,48},{64,72... | collective-permute-start | bytes 1572872 | tf_op jit(solution)/shard_map/ppermute | solution.py:374

commit v9 on v8

--- a/solution.py
+++ b/solution.py
@@ -10,9 +10,9 @@
 WINDOW = 32
 TILE = 64
 PAD = 16
-GROUP = 12
+GROUP = 8
 ZERO_TILE = WINDOW * GROUP
-STORE = (ZERO_TILE + 8, TILE, 128)
+STORE = (ZERO_TILE + 1, TILE, 128)
 ALL, EARLY, LOW, LOW_X = range(4)
 LISTS = (4, 8, 128)
 
@@ -24,7 +24,6 @@
             tile = ref[pl.ds((row * 4 + pair) * TILE, TILE), :]
             store[base + pair] = tile
             store[base + 4 + pair] = pltpu.roll(tile, 64, 1)
-            store[base + 8 + pair] = tile
 
 
 def from_pieces(x_ref, rows, sems, starts):
@@ -66,7 +65,6 @@
     core = lax.rem(lax.axis_index("rows"), 2)
     zeros = jnp.zeros((TILE, 128), jnp.bfloat16)
     store[ZERO_TILE] = zeros
-    store[ZERO_TILE + 4] = zeros
     fill(store, 1 + core, near_ref)
     fill(store, 2 - core, far_ref)
     for copy in copies:
@@ -105,7 +103,7 @@
         for q in range(8):
             wanted = highest(jnp.where(slot == (mine ^ q), own, -1))
             match = (found == wanted) & (wanted >= 0) & (row >= 0)
-            tile = highest(jnp.where(match, row * GROUP + side, -1))
+            tile = highest(jnp.where(match, row * GROUP + (side ^ (q % 2 * 4)), -1))
             result = jnp.where((slot == q) & (tile >= 0), tile, result)
         return result
 
@@ -116,7 +114,8 @@
     lists_ref[ALL] = everything
     lists_ref[EARLY] = jnp.where(source < HALF, ZERO_TILE, everything)
     lists_ref[LOW] = tiles(own_columns, lane % 8)
-    low_x = highest(jnp.where(own_columns == lane % 8, own_row * GROUP + side, -1))
+    right = (lane % 8 + lane // 8) % 2 * 4
+    low_x = highest(jnp.where(own_columns == lane % 8, own_row * GROUP + (side ^ right), -1))
     lists_ref[LOW_X] = jnp.where(low_x >= 0, low_x, ZERO_TILE)
 
 
@@ -130,7 +129,7 @@
     def tile(p, b):
         if b is None:
             return jnp.zeros((TILE, 128), jnp.bfloat16)
-        return jnp.where(left, store[tiles[2 * p, b]], store[tiles[2 * p + 1, b] + 4])
+        return jnp.where(left, store[tiles[2 * p, b]], store[tiles[2 * p + 1, b]])
 
     total = None
     for k in range(0, len(sources), 4):
@@ -163,7 +162,7 @@
         found = [ZERO_TILE if b is None else own_tiles[0, b] for b in sources]
         x = jnp.concatenate(
             [
-                jnp.where(left, store[found[k]], store[found[k + 1] + 4])
+                jnp.where(left, store[found[k]], store[found[k + 1]])
                 for k in range(0, len(sources), 2)
             ],
             axis=1,
@@ -195,8 +194,12 @@
     return put
 
 
-def waits_longest():
+def waits_for_near():
     return (lax.axis_index("rows") == 0) & (lax.axis_index("rep") != 0)
+
+
+def waits():
+    return waits_for_near() | (lax.axis_index("rows") == 1)
 
 
 def pack_kernel(
@@ -236,7 +239,7 @@
     def _():
         pack(far, far_rows, far_ref)
 
-    @pl.when(waits_longest())
+    @pl.when(waits())
     def _():
         own(near_ref, far_ref, cols_in, counts_in, lists_ref, store, cols_ref, counts_ref, own_sems)
 
@@ -247,7 +250,7 @@
 
 
 def own_kernel(near_ref, far_ref, cols_in, counts_in, _, __, lists_ref, store, cols_ref, counts_ref, sems):
-    @pl.when(jnp.logical_not(waits_longest()))
+    @pl.when(jnp.logical_not(waits()))
     def _():
         own(near_ref, far_ref, cols_in, counts_in, lists_ref, store, cols_ref, counts_ref, sems)
 
@@ -285,12 +288,12 @@
     def put(i, block):
         near[i] = block
 
-    @pl.when(waits_longest())
+    @pl.when(waits_for_near())
     def _():
         low_halo_squares(lists_ref, store, rounded(squares_ref, early_ref))
         cubes(lists_ref[ALL], store, squares_ref, put)
 
-    @pl.when(jnp.logical_not(waits_longest()))
+    @pl.when(jnp.logical_not(waits_for_near()))
     def _():
         tiles = half_list(lists_ref, 1 + core)
         squares(tiles, store, 1 + core, rounded(squares_ref))
@@ -303,9 +306,8 @@
         def put_far(i, block):
             far[i] = block
 
-        tiles = half_list(lists_ref, 2 - core)
-        squares(tiles, store, 2 - core, rounded(squares_ref))
-        cubes(tiles, store, squares_ref, put_far)
+        low_halo_squares(lists_ref, store, rounded(squares_ref, early_ref))
+        cubes(lists_ref[ALL], store, squares_ref, put_far)
         late_out.start()
         late_out.wait()
 

time: 26.9 us -> 26.7 us (level); the launches traced: 26.7 us -> 26.2 us
  starting transfers between devices: 19.2 us -> 16.7 us
  waiting for transfers between devices: 0.01 us -> 1.47 us
  Pallas kernels: 7.41 us -> 7.93 us
    ppermute x1, starting transfers between devices: 4.51 us -> 2.02 us  [local(): near_halo = lax.ppermute(near, 'rows', to_chip)]
    ppermute x1, waiting for transfers between devices: 0.01 us -> 1.46 us  [local(): far_halo = lax.ppermute(far, 'rows', to_core)]
    pallas_call x5, Pallas kernels: 7.41 us -> 7.93 us  [call(): pl.pallas_call(kernel, out_shape=out_shape, in_specs=in_specs, out_specs=...]
  transfers between devices with their start and end apart: 2 -> 2, of which waited for: 0 -> 1; matrix products, arithmetic and copies ran while one was open for 0% -> 0% of each run, Pallas kernels for 7% -> 1%
where the time goes in v9:
time: 26.7 us; the launch traced here: 26.2 us
  starting transfers between devices  16.7 us (63%)
  Pallas kernels  7.93 us (30%)
  waiting for transfers between devices  1.47 us (6%)
    ppermute x1, starting transfers between devices, local(): far_halo = lax.ppermute(far, 'rows', to_core)  14.7 us
    pallas_call x5, Pallas kernels, call(): pl.pallas_call(kernel, out_shape=out_shape, in_specs=in_specs, out_specs=...  7.93 us
    ppermute x1, starting transfers between devices, local(): near_halo = lax.ppermute(near, 'rows', to_chip)  2.02 us
    ppermute x1, waiting for transfers between devices, local(): far_halo = lax.ppermute(far, 'rows', to_core)  1.46 us
  transfers between devices with their start and end apart: 2, of which 1 were waited for; matrix products, arithmetic and copies ran while one was open for 0% of the time, Pallas kernels for 1%

profile of v9, /device:TPU:1, one launch (start us, length us, event | category | flops | bytes accessed | tf_op | source)
XLA Modules:
  0.0 26.2 jit_solution(5216249120695149913)
XLA Ops:
  0.0 4.3 %pack.1 = (bf16[2064,128]{1,0:T(8,128)(2,1)S(1)}, bf16[2048,128]{1,0:T(8,128)(2,1)S(1)}, s32[4,8,128]{2,1,0:T(8,128)S(1)}, bf16[257,64,128]{2,1,0:T(8,128)(2,1)S(1)}, f32[8,64,512]{2,1,0:T(8,128)S(1)}) custom-call(bf16[16,8,64,64]{3,2,1,0:T(8,128)(2,1)} %x_ref.3, s32[8,1536]{1,0:T(8,128)} %bitcast.2, s32[12,128]{1,0:T(8,128)} %bitcast.4), custom_call_target="tpu_custom_call" | custom-call | tf_op jit(solution)/shard_map/pack/pallas_call | solution.py:330
  4.3 2.0 %collective-permute-start = (bf16[2064,128]{1,0:T(8,128)(2,1)S(1)}, bf16[2064,128]{1,0:T(8,128)(2,1)S(1)}, u32[]{:S(2)}, u32[]{:S(2)}) collective-permute-start(bf16[2064,128]{1,0:T(8,128)(2,1)S(1)} %get-tuple-element.15.near_ref), channel_id=1, source_target_pairs={{0,760},{8,16},{16,8},{24,32},{32,24},{40,48},{48,40},{56,64},{64,... | collective-permute-start | bytes 1585160 | tf_op jit(solution)/shard_map/ppermute | solution.py:375
  6.4 14.7 %collective-permute-start.1 = (bf16[2048,128]{1,0:T(8,128)(2,1)S(1)}, bf16[2048,128]{1,0:T(8,128)(2,1)S(1)}, u32[]{:S(2)}, u32[]{:S(2)}) collective-permute-start(bf16[2048,128]{1,0:T(8,128)(2,1)S(1)} %rest.1.far_ref), channel_id=1, source_target_pairs={{0,8},{8,0},{16,24},{24,16},{32,40},{40,32},{48,56},{56,48},{64,72... | collective-permute-start | bytes 1572872 | tf_op jit(solution)/shard_map/ppermute | solution.py:376
  21.1 1.5 %collective-permute-done.1.halo_ref = bf16[2048,128]{1,0:T(8,128)(2,1)S(1)} collective-permute-done((bf16[2048,128]{1,0:T(8,128)(2,1)S(1)}, bf16[2048,128]{1,0:T(8,128)(2,1)S(1)}, u32[]{:S(2)}, u32[]{:S(2)}) %collective-permute-start.1) | collective-permute-done | bytes 524320 | tf_op jit(solution)/shard_map/ppermute | solution.py:376
  22.6 0.3 far_half.1
  22.9 0.0 collective-permute-done.halo_ref
  22.9 3.3 %near_half.1 = (bf16[16,1,64,64]{3,2,1,0:T(8,128)(2,1)}, bf16[257,64,128]{2,1,0:T(8,128)(2,1)S(1)}) custom-call(s32[4,8,128]{2,1,0:T(8,128)S(1)} %get-tuple-element.19.lists_ref, bf16[2064,128]{1,0:T(8,128)(2,1)S(1)} %collective-permute-done.halo_ref, bf16[8,64,64]{2,1,0:T(8,128)(2,1)S(1)} %get-tuple-element.21.far_in, ...), custom_call_target="tpu_custom_call", output_to_operand_aliasing={{1}: (4, {})} | custom-call | tf_op jit(solution)/shard_map/near_half/pallas_call | solution.py:330
  (2 shorter events, 0.1 us)
Async XLA Ops:
  4.3 18.6 %collective-permute-start = (bf16[2064,128]{1,0:T(8,128)(2,1)S(1)}, bf16[2064,128]{1,0:T(8,128)(2,1)S(1)}, u32[]{:S(2)}, u32[]{:S(2)}) collective-permute-start(bf16[2064,128]{1,0:T(8,128)(2,1)S(1)} %get-tuple-element.15.near_ref), channel_id=1, source_target_pairs={{0,760},{8,16},{16,8},{24,32},{32,24},{40,48},{48,40},{56,64},{64,... | collective-permute-start | bytes 1585160 | tf_op jit(solution)/shard_map/ppermute | solution.py:375
  6.4 16.2 %collective-permute-start.1 = (bf16[2048,128]{1,0:T(8,128)(2,1)S(1)}, bf16[2048,128]{1,0:T(8,128)(2,1)S(1)}, u32[]{:S(2)}, u32[]{:S(2)}) collective-permute-start(bf16[2048,128]{1,0:T(8,128)(2,1)S(1)} %rest.1.far_ref), channel_id=1, source_target_pairs={{0,8},{8,0},{16,24},{24,16},{32,40},{40,32},{48,56},{56,48},{64,72... | collective-permute-start | bytes 1572872 | tf_op jit(solution)/shard_map/ppermute | solution.py:376

commit v10 on v9

--- a/solution.py
+++ b/solution.py
@@ -154,19 +154,24 @@
             put(i, n, product(x, tiles, store, [i * 8 + b for b in range(8)], n))
 
 
-def low_halo_squares(lists_ref, store, put):
-    tiles, own_tiles = lists_ref[LOW], lists_ref[LOW_X]
+def low_halo_sources(i):
+    return [i * 8 + w for w in range(i, HALF)] + [None] * (i % 2)
+
+
+def low_halo_left(lists_ref, store, out_ref):
+    own_tiles = lists_ref[LOW_X]
     left = lax.broadcasted_iota(jnp.int16, (TILE, 128), 1) < 64
     for i in range(HALF):
-        sources = [i * 8 + w for w in range(i, HALF)] + [None] * (i % 2)
-        found = [ZERO_TILE if b is None else own_tiles[0, b] for b in sources]
-        x = jnp.concatenate(
-            [
-                jnp.where(left, store[found[k]], store[found[k + 1]])
-                for k in range(0, len(sources), 2)
-            ],
-            axis=1,
-        )
+        found = [ZERO_TILE if b is None else own_tiles[0, b] for b in low_halo_sources(i)]
+        for k in range(0, len(found), 2):
+            out_ref[i, :, k * 64 : k * 64 + 128] = jnp.where(left, store[found[k]], store[found[k + 1]])
+
+
+def low_halo_squares(lists_ref, left_ref, store, put):
+    tiles = lists_ref[LOW]
+    for i in range(HALF):
+        sources = low_halo_sources(i)
+        x = left_ref[i, :, : len(sources) * 64]
         for n in range(2):
             put(i, n, product(x, tiles, store, sources, n))
 
@@ -211,6 +216,7 @@
     lists_ref,
     store,
     early_ref,
+    left_ref,
     near_rows,
     far_rows,
     near_sems,
@@ -247,6 +253,7 @@
             early_ref[i, :, n * 256 : (n + 1) * 256] = total
 
         squares(lists_ref[EARLY], store, 1, put)
+        low_halo_left(lists_ref, store, left_ref)
 
 
 def own_kernel(near_ref, far_ref, cols_in, counts_in, _, __, lists_ref, store, cols_ref, counts_ref, sems):
@@ -270,7 +277,9 @@
         cubes(tiles, store, squares_ref, put)
 
 
-def near_kernel(lists_ref, halo_ref, far_in, early_ref, _, out_ref, store, squares_ref, near, far, sems):
+def near_kernel(
+    lists_ref, halo_ref, far_in, early_ref, left_ref, _, out_ref, store, squares_ref, near, far, sems
+):
     me = lax.axis_index("rows")
     core = lax.rem(me, 2)
     near_at = out_ref.at[pl.ds(core * HALF, HALF), 0]
@@ -290,7 +299,7 @@
 
     @pl.when(waits_for_near())
     def _():
-        low_halo_squares(lists_ref, store, rounded(squares_ref, early_ref))
+        low_halo_squares(lists_ref, left_ref, store, rounded(squares_ref, early_ref))
         cubes(lists_ref[ALL], store, squares_ref, put)
 
     @pl.when(jnp.logical_not(waits_for_near()))
@@ -306,7 +315,7 @@
         def put_far(i, block):
             far[i] = block
 
-        low_halo_squares(lists_ref, store, rounded(squares_ref, early_ref))
+        low_halo_squares(lists_ref, left_ref, store, rounded(squares_ref, early_ref))
         cubes(lists_ref[ALL], store, squares_ref, put_far)
         late_out.start()
         late_out.wait()
@@ -353,13 +362,13 @@
     cols, counts = (pltpu.with_memory_space_constraint(x, pltpu.HBM) for x in (cols, counts))
     pattern = [pltpu.VMEM(cols.shape, i32), pltpu.VMEM(counts.shape, i32), pltpu.SemaphoreType.DMA((2,))]
     stored = [jax.ShapeDtypeStruct(LISTS, i32), jax.ShapeDtypeStruct(STORE, bf16)]
-    near, far, lists, store, early = call(
+    near, far, lists, store, early, left = call(
         pack_kernel,
         "pack",
         [block_values, cols, counts],
         [hbm()] * 3,
-        packed + stored + [jax.ShapeDtypeStruct((HALF, 64, 512), jnp.float32)],
-        [vmem()] * 5,
+        packed + stored + [jax.ShapeDtypeStruct((HALF, 64, 512), kind) for kind in (jnp.float32, bf16)],
+        [vmem()] * 6,
         rows * 2 + sems * 2 + pattern,
     )
     far = call(
@@ -398,12 +407,12 @@
     result, _ = call(
         near_kernel,
         "near_half",
-        [lists, near_halo, far_result, early, store],
-        [vmem()] * 5,
+        [lists, near_halo, far_result, early, left, store],
+        [vmem()] * 6,
         [jax.ShapeDtypeStruct((2 * HALF, 1, 64, 64), bf16), stored[1]],
         [hbm(), vmem()],
         scratch + [pltpu.VMEM((HALF, 64, 64), bf16)] * 2 + [pltpu.SemaphoreType.DMA((2,))],
-        {4: 1},
+        {5: 1},
     )
     return result
 

time: 26.7 us -> 26.7 us (level)
  no operation moved by 1% of the time
where the time goes in v10:
time: 26.7 us; the launch traced here: 26.1 us
  starting transfers between devices  16.7 us (63%)
  Pallas kernels  7.93 us (30%)
  waiting for transfers between devices  1.47 us (6%)
    ppermute x1, starting transfers between devices, local(): far_halo = lax.ppermute(far, 'rows', to_core)  14.7 us
    pallas_call x5, Pallas kernels, call(): pl.pallas_call(kernel, out_shape=out_shape, in_specs=in_specs, out_specs=...  7.93 us
    ppermute x1, starting transfers between devices, local(): near_halo = lax.ppermute(near, 'rows', to_chip)  2 us
    ppermute x1, waiting for transfers between devices, local(): far_halo = lax.ppermute(far, 'rows', to_core)  1.46 us
  transfers between devices with their start and end apart: 2, of which 1 were waited for; matrix products, arithmetic and copies ran while one was open for 0% of the time, Pallas kernels for 1%

profile of v10, /device:TPU:1, one launch (start us, length us, event | category | flops | bytes accessed | tf_op | source)
XLA Modules:
  0.0 26.1 jit_solution(16018370062848136496)
XLA Ops:
  0.0 4.3 %pack.1 = (bf16[2064,128]{1,0:T(8,128)(2,1)S(1)}, bf16[2048,128]{1,0:T(8,128)(2,1)S(1)}, s32[4,8,128]{2,1,0:T(8,128)S(1)}, bf16[257,64,128]{2,1,0:T(8,128)(2,1)S...) custom-call(bf16[16,8,64,64]{3,2,1,0:T(8,128)(2,1)} %x_ref.3, s32[8,1536]{1,0:T(8,128)} %bitcast.2, ...), custom_call_target="tpu_custom_call" | custom-call | tf_op jit(solution)/shard_map/pack/pallas_call | solution.py:339
  4.3 2.0 %collective-permute-start = (bf16[2064,128]{1,0:T(8,128)(2,1)S(1)}, bf16[2064,128]{1,0:T(8,128)(2,1)S(1)}, u32[]{:S(2)}, u32[]{:S(2)}) collective-permute-start(bf16[2064,128]{1,0:T(8,128)(2,1)S(1)} %get-tuple-element.16.near_ref), channel_id=1, source_target_pairs={{0,760},{8,16},{16,8},{24,32},{32,24},{40,48},{48,40},{56,64},{64,... | collective-permute-start | bytes 1585160 | tf_op jit(solution)/shard_map/ppermute | solution.py:384
  6.4 14.7 %collective-permute-start.1 = (bf16[2048,128]{1,0:T(8,128)(2,1)S(1)}, bf16[2048,128]{1,0:T(8,128)(2,1)S(1)}, u32[]{:S(2)}, u32[]{:S(2)}) collective-permute-start(bf16[2048,128]{1,0:T(8,128)(2,1)S(1)} %rest.1.far_ref), channel_id=1, source_target_pairs={{0,8},{8,0},{16,24},{24,16},{32,40},{40,32},{48,56},{56,48},{64,72... | collective-permute-start | bytes 1572872 | tf_op jit(solution)/shard_map/ppermute | solution.py:385
  21.1 1.5 %collective-permute-done.1.halo_ref = bf16[2048,128]{1,0:T(8,128)(2,1)S(1)} collective-permute-done((bf16[2048,128]{1,0:T(8,128)(2,1)S(1)}, bf16[2048,128]{1,0:T(8,128)(2,1)S(1)}, u32[]{:S(2)}, u32[]{:S(2)}) %collective-permute-start.1) | collective-permute-done | bytes 524320 | tf_op jit(solution)/shard_map/ppermute | solution.py:385
  22.6 0.3 far_half.1
  22.9 0.0 collective-permute-done.halo_ref
  22.9 3.3 %near_half.1 = (bf16[16,1,64,64]{3,2,1,0:T(8,128)(2,1)}, bf16[257,64,128]{2,1,0:T(8,128)(2,1)S(1)}) custom-call(s32[4,8,128]{2,1,0:T(8,128)S(1)} %get-tuple-element.20.lists_ref, bf16[2064,128]{1,0:T(8,128)(2,1)S(1)} %collective-permute-done.halo_ref, bf16[8,64,64]{2,1,0:T(8,128)(2,1)S(1)} %get-tuple-element.22.far_in, ...), custom_call_target="tpu_custom_call", output_to_operand_aliasing={{1}: (5, {})} | custom-call | tf_op jit(solution)/shard_map/near_half/pallas_call | solution.py:339
  (2 shorter events, 0.1 us)
Async XLA Ops:
  4.3 18.5 %collective-permute-start = (bf16[2064,128]{1,0:T(8,128)(2,1)S(1)}, bf16[2064,128]{1,0:T(8,128)(2,1)S(1)}, u32[]{:S(2)}, u32[]{:S(2)}) collective-permute-start(bf16[2064,128]{1,0:T(8,128)(2,1)S(1)} %get-tuple-element.16.near_ref), channel_id=1, source_target_pairs={{0,760},{8,16},{16,8},{24,32},{32,24},{40,48},{48,40},{56,64},{64,... | collective-permute-start | bytes 1585160 | tf_op jit(solution)/shard_map/ppermute | solution.py:384
  6.4 16.2 %collective-permute-start.1 = (bf16[2048,128]{1,0:T(8,128)(2,1)S(1)}, bf16[2048,128]{1,0:T(8,128)(2,1)S(1)}, u32[]{:S(2)}, u32[]{:S(2)}) collective-permute-start(bf16[2048,128]{1,0:T(8,128)(2,1)S(1)} %rest.1.far_ref), channel_id=1, source_target_pairs={{0,8},{8,0},{16,24},{24,16},{32,40},{40,32},{48,56},{56,48},{64,72... | collective-permute-start | bytes 1572872 | tf_op jit(solution)/shard_map/ppermute | solution.py:385

commit v11 on v10

--- a/solution.py
+++ b/solution.py
@@ -6,7 +6,7 @@
 from jax.sharding import PartitionSpec as P
 
 HALF = 8
-PIECE = 4
+PIECES = ((0, 6), (6, 2))
 WINDOW = 32
 TILE = 64
 PAD = 16
@@ -26,17 +26,17 @@
             store[base + 4 + pair] = pltpu.roll(tile, 64, 1)
 
 
-def from_pieces(x_ref, rows, sems, starts):
+def from_pieces(x_ref, rows, sems, base):
     return [
-        pltpu.make_async_copy(x_ref.at[pl.ds(start, PIECE)], rows.at[pl.ds(n * PIECE, PIECE)], sems.at[n])
-        for n, start in enumerate(starts)
+        pltpu.make_async_copy(x_ref.at[pl.ds(base + at, size)], rows.at[pl.ds(at, size)], sems.at[n])
+        for n, (at, size) in enumerate(PIECES)
     ]
 
 
 def pack(copies, rows, out_ref):
-    for n, copy in enumerate(copies):
+    for copy, (first, size) in zip(copies, PIECES):
         copy.wait()
-        for row in range(n * PIECE, (n + 1) * PIECE):
+        for row in range(first, first + size):
             for pair in range(4):
                 at = pl.ds((row * 4 + pair) * TILE, TILE)
                 blocks = [rows[row, 2 * pair + side] for side in range(2)]
@@ -49,7 +49,7 @@
 
     @pl.when(me == lax.axis_size("rows") - 1)
     def _():
-        far = from_pieces(x_ref, far_rows, far_sems, ((1 - core) * HALF, (1 - core) * HALF + PIECE))
+        far = from_pieces(x_ref, far_rows, far_sems, (1 - core) * HALF)
         for copy in far:
             copy.start()
         pack(far, far_rows, far_ref)
@@ -228,8 +228,8 @@
     me = lax.axis_index("rows")
     core = lax.rem(me, 2)
     late = me == lax.axis_size("rows") - 1
-    near = from_pieces(x_ref, near_rows, near_sems, (core * HALF, core * HALF + PIECE))
-    far = from_pieces(x_ref, far_rows, far_sems, ((1 - core) * HALF, (1 - core) * HALF + PIECE))
+    near = from_pieces(x_ref, near_rows, near_sems, core * HALF)
+    far = from_pieces(x_ref, far_rows, far_sems, (1 - core) * HALF)
     for copy in near:
         copy.start()
 
@@ -356,7 +356,7 @@
     bf16, i32 = jnp.bfloat16, jnp.int32
     block_values = pltpu.with_memory_space_constraint(block_values, pltpu.HBM)
     rows = [pltpu.VMEM((HALF, 8, 64, 64), bf16)]
-    sems = [pltpu.SemaphoreType.DMA((HALF // PIECE,))]
+    sems = [pltpu.SemaphoreType.DMA((len(PIECES),))]
     packed = [jax.ShapeDtypeStruct((HALF * 4 * TILE + pad, 128), bf16) for pad in (PAD, 0)]
     cols, counts = pattern_cols.T, pattern_counts.reshape(-1, 128)
     cols, counts = (pltpu.with_memory_space_constraint(x, pltpu.HBM) for x in (cols, counts))

time: 26.7 us -> 26.7 us (level)
  no operation moved by 1% of the time
where the time goes in v11:
time: 26.7 us; the launch traced here: 26.2 us
  starting transfers between devices  16.7 us (63%)
  Pallas kernels  7.97 us (30%)
  waiting for transfers between devices  1.47 us (6%)
    ppermute x1, starting transfers between devices, local(): far_halo = lax.ppermute(far, 'rows', to_core)  14.7 us
    pallas_call x5, Pallas kernels, call(): pl.pallas_call(kernel, out_shape=out_shape, in_specs=in_specs, out_specs=...  7.97 us
    ppermute x1, starting transfers between devices, local(): near_halo = lax.ppermute(near, 'rows', to_chip)  2 us
    ppermute x1, waiting for transfers between devices, local(): far_halo = lax.ppermute(far, 'rows', to_core)  1.46 us
  transfers between devices with their start and end apart: 2, of which 1 were waited for; matrix products, arithmetic and copies ran while one was open for 0% of the time, Pallas kernels for 1%

profile of v11, /device:TPU:1, one launch (start us, length us, event | category | flops | bytes accessed | tf_op | source)
XLA Modules:
  0.0 26.2 jit_solution(1921434003938003612)
XLA Ops:
  0.0 4.4 %pack.1 = (bf16[2064,128]{1,0:T(8,128)(2,1)S(1)}, bf16[2048,128]{1,0:T(8,128)(2,1)S(1)}, s32[4,8,128]{2,1,0:T(8,128)S(1)}, bf16[257,64,128]{2,1,0:T(8,128)(2,1)S...) custom-call(bf16[16,8,64,64]{3,2,1,0:T(8,128)(2,1)} %x_ref.3, s32[8,1536]{1,0:T(8,128)} %bitcast.2, ...), custom_call_target="tpu_custom_call" | custom-call | tf_op jit(solution)/shard_map/pack/pallas_call | solution.py:339
  4.4 2.0 %collective-permute-start = (bf16[2064,128]{1,0:T(8,128)(2,1)S(1)}, bf16[2064,128]{1,0:T(8,128)(2,1)S(1)}, u32[]{:S(2)}, u32[]{:S(2)}) collective-permute-start(bf16[2064,128]{1,0:T(8,128)(2,1)S(1)} %get-tuple-element.16.near_ref), channel_id=1, source_target_pairs={{0,760},{8,16},{16,8},{24,32},{32,24},{40,48},{48,40},{56,64},{64,... | collective-permute-start | bytes 1585160 | tf_op jit(solution)/shard_map/ppermute | solution.py:384
  6.4 14.7 %collective-permute-start.1 = (bf16[2048,128]{1,0:T(8,128)(2,1)S(1)}, bf16[2048,128]{1,0:T(8,128)(2,1)S(1)}, u32[]{:S(2)}, u32[]{:S(2)}) collective-permute-start(bf16[2048,128]{1,0:T(8,128)(2,1)S(1)} %rest.1.far_ref), channel_id=1, source_target_pairs={{0,8},{8,0},{16,24},{24,16},{32,40},{40,32},{48,56},{56,48},{64,72... | collective-permute-start | bytes 1572872 | tf_op jit(solution)/shard_map/ppermute | solution.py:385
  21.2 1.5 %collective-permute-done.1.halo_ref = bf16[2048,128]{1,0:T(8,128)(2,1)S(1)} collective-permute-done((bf16[2048,128]{1,0:T(8,128)(2,1)S(1)}, bf16[2048,128]{1,0:T(8,128)(2,1)S(1)}, u32[]{:S(2)}, u32[]{:S(2)}) %collective-permute-start.1) | collective-permute-done | bytes 524320 | tf_op jit(solution)/shard_map/ppermute | solution.py:385
  22.7 0.3 far_half.1
  22.9 0.0 collective-permute-done.halo_ref
  23.0 3.3 %near_half.1 = (bf16[16,1,64,64]{3,2,1,0:T(8,128)(2,1)}, bf16[257,64,128]{2,1,0:T(8,128)(2,1)S(1)}) custom-call(s32[4,8,128]{2,1,0:T(8,128)S(1)} %get-tuple-element.20.lists_ref, bf16[2064,128]{1,0:T(8,128)(2,1)S(1)} %collective-permute-done.halo_ref, bf16[8,64,64]{2,1,0:T(8,128)(2,1)S(1)} %get-tuple-element.22.far_in, ...), custom_call_target="tpu_custom_call", output_to_operand_aliasing={{1}: (5, {})} | custom-call | tf_op jit(solution)/shard_map/near_half/pallas_call | solution.py:339
  (2 shorter events, 0.1 us)
Async XLA Ops:
  4.4 18.6 %collective-permute-start = (bf16[2064,128]{1,0:T(8,128)(2,1)S(1)}, bf16[2064,128]{1,0:T(8,128)(2,1)S(1)}, u32[]{:S(2)}, u32[]{:S(2)}) collective-permute-start(bf16[2064,128]{1,0:T(8,128)(2,1)S(1)} %get-tuple-element.16.near_ref), channel_id=1, source_target_pairs={{0,760},{8,16},{16,8},{24,32},{32,24},{40,48},{48,40},{56,64},{64,... | collective-permute-start | bytes 1585160 | tf_op jit(solution)/shard_map/ppermute | solution.py:384
  6.4 16.3 %collective-permute-start.1 = (bf16[2048,128]{1,0:T(8,128)(2,1)S(1)}, bf16[2048,128]{1,0:T(8,128)(2,1)S(1)}, u32[]{:S(2)}, u32[]{:S(2)}) collective-permute-start(bf16[2048,128]{1,0:T(8,128)(2,1)S(1)} %rest.1.far_ref), channel_id=1, source_target_pairs={{0,8},{8,0},{16,24},{24,16},{32,40},{40,32},{48,56},{56,48},{64,72... | collective-permute-start | bytes 1572872 | tf_op jit(solution)/shard_map/ppermute | solution.py:385
